TPU v7x, 32 devices: a whole 2x2x4 slice. The times are simulated.
32 devices in a mesh: groups: 2 (over y), tp: 4 (over z), seq: 4 (over x, core).
Axes of the slice: x: 2, y: 2, z: 4, core: 2. Of those that a mesh axis runs over, the one named last changes fastest.
Arguments:
- tokens_values: bfloat16 [1024, 8192], P(('groups', 'seq'), 'tp'), parts along dimension 0, may hold values from -1 to 1
- tokens_scales: float32 [1024, 64], P(('groups', 'seq'), 'tp'), parts along dimension 0, may hold values from 0.25 to 4
- gate_weight: bfloat16 [8192, 16384], P('seq', 'tp'), may hold values from -0.0625 to 0.0625
- up_weight: bfloat16 [8192, 16384], P('seq', 'tp'), may hold values from -0.0625 to 0.0625
- down_weight: bfloat16 [16384, 8192], P('tp', 'seq'), may hold values from -0.0625 to 0.0625
Outputs:
- mixed_values: bfloat16 [1024, 8192], P(('groups', 'seq'), 'tp'), parts along dimension 0
- mixed_scales: float32 [1024, 64], P(('groups', 'seq'), 'tp'), parts along dimension 0
There are 2 independent parts, one for each index of `groups`. A program takes and returns all parts, laid end to end along the dimension named above; an argument that names none is the same for every part. Nothing has to cross between parts.
All inputs are finite; a program needn't handle non-finite values.
Results may differ from a plain program's by a relative error of at most 0.02.
Values may be sent and summed in bfloat16 or wider, within the bound.
No kernel may reach another device: no remote copies, remote signals or barrier semaphores. Data moves between devices by JAX's collectives and lax.ppermute only.
A program may use at most 512 MiB of HBM per device.

v0:
```python
import jax
import jax.numpy as jnp
from jax import lax
from jax.sharding import PartitionSpec as P


def blocks(array):
    return array.reshape(array.shape[0], array.shape[1] // 128, 128)


def block_scale(array):
    return jnp.max(jnp.abs(blocks(array)), axis=2) + 1e-06


def expand(values, scales):
    return (blocks(values.astype(jnp.float32)) * scales[:, :, None]).reshape(values.shape)


def shards(tokens_values, tokens_scales, gate_weight, up_weight, down_weight):
    values, scales = (
        lax.all_gather(tokens_values, "tp", axis=1, tiled=True),
        lax.all_gather(tokens_scales.astype(jnp.bfloat16), "tp", axis=1, tiled=True).astype(
            tokens_scales.dtype
        ),
    )
    rows = values.shape[0]
    width = values.shape[1]
    inputs = expand(values, scales).astype(jnp.bfloat16)
    gate = jnp.dot(
        inputs,
        lax.all_gather(gate_weight, "seq", axis=0, tiled=True),
        preferred_element_type=jnp.float32,
    )
    up = jnp.dot(
        inputs,
        lax.all_gather(up_weight, "seq", axis=0, tiled=True),
        preferred_element_type=jnp.float32,
    )
    hidden = (jax.nn.silu(gate) * up).astype(jnp.bfloat16)
    partial_sum = jnp.dot(
        hidden,
        lax.all_gather(down_weight, "seq", axis=1, tiled=True),
        preferred_element_type=jnp.float32,
    )
    scale = block_scale(partial_sum)
    quant = (blocks(partial_sum) / scale[:, :, None]).reshape(rows, width).astype(jnp.bfloat16)
    tp_count = lax.axis_size("tp")
    got_values, got_scales = (
        lax.all_to_all(quant, "tp", split_axis=1, concat_axis=0, tiled=True),
        lax.all_to_all(
            scale.astype(jnp.bfloat16), "tp", split_axis=1, concat_axis=0, tiled=True
        ).astype(scale.dtype),
    )
    shard = width // tp_count
    terms = expand(got_values, got_scales)
    total = jnp.sum(terms.reshape(tp_count, rows, shard), axis=0)
    mixed_scales = block_scale(total)
    mixed_values = (
        (blocks(total) / mixed_scales[:, :, None]).reshape(total.shape).astype(jnp.bfloat16)
    )
    return (mixed_values, mixed_scales)


def solution(mesh):
    placed = (
        P(("groups", "seq"), "tp"),
        P(("groups", "seq"), "tp"),
        P("seq", "tp"),
        P("seq", "tp"),
        P("tp", "seq"),
    )
    return jax.shard_map(
        shards,
        mesh=mesh,
        in_specs=placed,
        out_specs=(P(("groups", "seq"), "tp"), P(("groups", "seq"), "tp")),
        check_vma=False,
    )
```

profile of v0, /device:TPU:1, one launch (start us, length us, event | category | flops | bytes accessed | tf_op | source)
XLA Modules:
  0.0 1350.3 jit_solution(10503948712991929397)
XLA Ops:
  7.2 0.7 all-gather.5.cloned.1.call-update
  7.9 0.7 all-gather.7.cloned.1.call-update
  8.7 0.7 all-gather.9.cloned.1.call-update
  9.4 0.5 all-gather.11.cloned.1.call-update
  10.1 11.3 all_gather.16
  21.5 36.4 %all-gather.5.cloned.1.call-done = bf16[128,8192]{1,0:T(8,128)(2,1)} async-done(((bf16[128,2048]{1,0:T(8,128)(2,1)}), bf16[128,8192]{1,0:T(8,128)(2,1)}) %all-gather.5.cloned.1.call-update) | async-done | bytes 2097168 | tf_op jit(solution)/shard_map/all_gather | solution.py:21
  57.9 393.6 %all-gather.7.cloned.1.call-done = bf16[8192,4096]{1,0:T(8,128)(2,1)} async-done(((bf16[2048,4096]{1,0:T(8,128)(2,1)}), bf16[8192,4096]{1,0:T(8,128)(2,1)}) %all-gather.7.cloned.1.call-update) | async-done | bytes 67108880 | tf_op jit(solution)/shard_map/all_gather | solution.py:31
  451.5 2.6 mul.29
  454.1 44.7 %fusion.16 = f32[128,4096]{1,0:T(8,128)} fusion(bf16[8192,4096]{1,0:T(8,128)(2,1)} %all-gather.7.cloned.1.call-done, f32[16,8,64,128]{3,2,1,0:T(8,128)} %bitcast.47, bf16[128,8192]{1,0:T(8,128)(2,1)S(1)} %copy-done.1), kind=kOutput, calls=%fused_computation.25 | convolution fusion | flops 8593080320 | bytes 75497472 | tf_op jit(solution)/shard_map/dot_general | solution.py:29
  498.8 347.0 %all-gather.9.cloned.1.call-done = bf16[8192,4096]{1,0:T(8,128)(2,1)} async-done(((bf16[2048,4096]{1,0:T(8,128)(2,1)}), bf16[8192,4096]{1,0:T(8,128)(2,1)}) %all-gather.9.cloned.1.call-update) | async-done | bytes 67108880 | tf_op jit(solution)/shard_map/all_gather | solution.py:36
  845.8 41.4 %fusion.clone.4 = bf16[128,4096]{1,0:T(8,128)(2,1)S(1)} fusion(bf16[8192,4096]{1,0:T(8,128)(2,1)} %all-gather.9.cloned.1.call-done, f32[128,4096]{1,0:T(8,128)} %fusion.16, f32[16,8,64,128]{3,2,1,0:T(8,128)} %bitcast.48, bf16[128,8192]{1,0:T(8,128)(2,1)S(1)} %copy-done.1), kind=kOutput, calls=%fused_computation.1.clone.clone.clone.1 | convolution fusion | flops 8596226048 | bytes 76546048 | tf_op jit(solution)/shard_map/dot_general | solution.py:34
  887.2 352.8 %all-gather.11.cloned.1.call-done = bf16[4096,8192]{1,0:T(8,128)(2,1)} async-done(((bf16[4096,2048]{1,0:T(8,128)(2,1)}), bf16[4096,8192]{1,0:T(8,128)(2,1)}) %all-gather.11.cloned.1.call-update) | async-done | bytes 67108880 | tf_op jit(solution)/shard_map/all_gather | solution.py:42
  1240.0 24.8 %fusion.1 = f32[128,8192]{1,0:T(8,128)} fusion(bf16[4096,8192]{1,0:T(8,128)(2,1)} %all-gather.11.cloned.1.call-done, bf16[128,4096]{1,0:T(8,128)(2,1)S(1)} %fusion.clone.4), kind=kOutput, calls=%fused_computation.2 | convolution fusion | flops 8589934592 | bytes 72351744 | tf_op jit(solution)/shard_map/dot_general | solution.py:40
  1264.8 2.6 abs_bitcast_fusion
  1267.3 2.7 copy.25
  1270.0 3.3 reduce_max.18
  1273.4 0.7 copy.17
  1274.1 4.3 all-to-all-start.1
  1278.4 1.1 div.27
  1279.6 1.0 copy-done
  1280.6 3.7 fusion.2
  1284.3 1.5 copy.39
  1285.8 4.5 all-to-all-start
  1290.5 2.6 mul.34
  1293.0 4.9 mul.35
  1297.9 40.1 %all-to-all-done = bf16[128,4,2048]{2,0,1:T(8,128)(2,1)S(1)} async-done(((bf16[128,4,2048]{2,0,1:T(8,128)(2,1)}), bf16[128,4,2048]{2,0,1:T(8,128)(2,1)S(1)}, u32[]{:S(2)}, u32[]{:S(2)}) %all-to-all-start) | async-done | bytes 2097184 | tf_op jit(solution)/shard_map/all_to_all | solution.py:49
  1338.0 2.9 fusion.4
  1341.0 0.2 copy.27
  1341.2 0.3 reduce_max.19
  1341.6 0.7 copy.20
  1342.2 0.3 div.30
  1342.6 1.2 fusion.10
  (17 shorter events, 0.6 us)
Async XLA Ops:
  7.2 50.7 %all-gather.5.cloned.1.call-start = ((), (), s32[]{:S(2)}) async-start(), calls=%async_computation.2 | async-start | bytes 2621440 | tf_op jit(solution)/shard_map/all_gather | solution.py:21
  7.9 443.6 %all-gather.7.cloned.1.call-start = ((), (), s32[]{:S(2)}) async-start(), calls=%async_computation.3 | async-start | bytes 83886080 | tf_op jit(solution)/shard_map/all_gather | solution.py:31
  8.6 837.2 %all-gather.9.cloned.1.call-start = ((), (), s32[]{:S(2)}) async-start(), calls=%async_computation.4 | async-start | bytes 83886080 | tf_op jit(solution)/shard_map/all_gather | solution.py:36
  9.4 0.7 copy-start.2
  9.4 1230.6 %all-gather.11.cloned.1.call-start = ((), (), s32[]{:S(2)}) async-start(), calls=%async_computation.5 | async-start | bytes 83886080 | tf_op jit(solution)/shard_map/all_gather | solution.py:42
  57.8 396.2 %copy-start.1 = (bf16[128,8192]{1,0:T(8,128)(2,1)S(1)}, bf16[128,8192]{1,0:T(8,128)(2,1)}, u32[]{:S(2)}) copy-start(bf16[128,8192]{1,0:T(8,128)(2,1)} %all-gather.5.cloned.1.call-done) | copy-start | bytes 6291460
  1274.1 11.7 all-to-all-start.1
  1278.4 2.2 copy-start
  1285.8 52.2 %all-to-all-start = ((bf16[128,4,2048]{2,0,1:T(8,128)(2,1)}), bf16[128,4,2048]{2,0,1:T(8,128)(2,1)S(1)}, u32[]{:S(2)}, u32[]{:S(2)}) async-start(bf16[128,4,2048]{2,0,1:T(8,128)(2,1)} %bitcast.52), calls=%async_computation | async-start | bytes 4194304 | tf_op jit(solution)/shard_map/all_to_all | solution.py:49
Sparse Core Ops, SparseCore 0:
  9.6 48.2 all-gather.4
  59.4 392.0 all-gather.6
  453.0 392.7 all-gather.8
  847.2 392.7 all-gather.10
where the time goes:
time: 1350 us
  waiting for transfers between devices  1170 us (87%)
  matrix products  111 us (8%)
  local copies, waits for them, and re-layouts  18.7 us (1%)
  other arithmetic  14.1 us (1%)
  between operations  13.9 us (1%)
    all_gather x1, waiting for transfers between devices, shards(): lax.all_gather(gate_weight, 'seq', axis=0, tiled=True)  394 us
    all_gather x1, waiting for transfers between devices, shards(): lax.all_gather(down_weight, 'seq', axis=1, tiled=True)  353 us
    all_gather x1, waiting for transfers between devices, shards(): lax.all_gather(up_weight, 'seq', axis=0, tiled=True)  347 us
    dot_general x1, matrix products, shards(): jnp.dot(inputs, lax.all_gather(gate_weight, 'seq', axis=0, tiled=True), p...  44.7 us
    dot_general x1, matrix products, shards(): jnp.dot(inputs, lax.all_gather(up_weight, 'seq', axis=0, tiled=True), pre...  41.4 us
    all_to_all x1, waiting for transfers between devices, shards(): lax.all_to_all(quant, 'tp', split_axis=1, concat_axis=0, tiled=True)  40.1 us
    all_gather x1, waiting for transfers between devices, shards(): lax.all_gather(tokens_values, 'tp', axis=1, tiled=True)  36.4 us
  transfers between devices with their start and end apart: 6, of which 5 were waited for; matrix products, arithmetic and copies ran while one was open for 8% of the time, Pallas kernels for 0%

commit v1 on v0

v1 whole, which is shorter than its diff:
```python
import jax
import jax.numpy as jnp
from jax import lax
from jax.sharding import PartitionSpec as P


def blocks(array):
    return array.reshape(array.shape[0], array.shape[1] // 128, 128)


def block_scale(array):
    return jnp.max(jnp.abs(blocks(array)), axis=2) + 1e-06


def expand(values, scales):
    return (blocks(values.astype(jnp.float32)) * scales[:, :, None]).reshape(values.shape)


def shards(tokens_values, tokens_scales, gate_weight, up_weight, down_weight):
    mine = expand(tokens_values, tokens_scales).astype(jnp.bfloat16)
    mine = lax.all_gather(mine, "tp", axis=1, tiled=True)
    inputs = lax.all_to_all(mine, "seq", split_axis=1, concat_axis=0, tiled=True)
    gate = jnp.dot(inputs, gate_weight, preferred_element_type=jnp.float32).astype(jnp.bfloat16)
    up = jnp.dot(inputs, up_weight, preferred_element_type=jnp.float32).astype(jnp.bfloat16)
    gate = lax.psum_scatter(gate, "seq", scatter_dimension=0, tiled=True).astype(jnp.float32)
    up = lax.psum_scatter(up, "seq", scatter_dimension=0, tiled=True).astype(jnp.float32)
    hidden = (jax.nn.silu(gate) * up).astype(jnp.bfloat16)
    hidden = lax.all_gather(hidden, "seq", axis=0, tiled=True)
    partial_sum = jnp.dot(hidden, down_weight, preferred_element_type=jnp.float32).astype(jnp.bfloat16)
    partial_sum = lax.all_to_all(partial_sum, "seq", split_axis=0, concat_axis=1, tiled=True)
    total = lax.psum_scatter(partial_sum, "tp", scatter_dimension=1, tiled=True).astype(jnp.float32)
    mixed_scales = block_scale(total)
    mixed_values = (
        (blocks(total) / mixed_scales[:, :, None]).reshape(total.shape).astype(jnp.bfloat16)
    )
    return (mixed_values, mixed_scales)


def solution(mesh):
    placed = (
        P(("groups", "seq"), "tp"),
        P(("groups", "seq"), "tp"),
        P("seq", "tp"),
        P("seq", "tp"),
        P("tp", "seq"),
    )
    return jax.shard_map(
        shards,
        mesh=mesh,
        in_specs=placed,
        out_specs=(P(("groups", "seq"), "tp"), P(("groups", "seq"), "tp")),
        check_vma=False,
    )
```

time: 1350 us -> 331 us (0.25)
  waiting for transfers between devices: 1170 us -> 201 us
  matrix products: 111 us -> 42.3 us
  blocking collectives: 11.3 us -> 56.3 us
    all_gather x4 -> x2, waiting for transfers between devices: 1130 us -> 83.1 us  [the longest x1 48.1 us: shards(): mine = lax.all_gather(mine, 'tp', axis=1, tiled=True)]
    reduce_scatter x0 -> x3, waiting for transfers between devices: none -> 118 us  [the longest x1 47.2 us: shards(): lax.psum_scatter(gate, 'seq', scatter_dimension=0, tiled=True)]
    dot_general x3, matrix products: 111 us -> 42.3 us  [the longest x1 14.4 us: shards(): jnp.dot(inputs, gate_weight, preferred_element_type=jnp.float32)]
    all_to_all x0 -> x2, blocking collectives: none -> 56.3 us  [the longest x1 28.9 us: shards(): lax.all_to_all(mine, 'seq', split_axis=1, concat_axis=0, tiled=True)]
    all_to_all x2 -> x0, waiting for transfers between devices: 40.1 us -> none  [the longest x1 40.1 us: shards(): lax.all_to_all(quant, 'tp', split_axis=1, concat_axis=0, tiled=True)]
  transfers between devices with their start and end apart: 6 -> 5, of which waited for: 5 -> 5; matrix products, arithmetic and copies ran while one was open for 8% -> 4% of each run, Pallas kernels for 0% -> 0%
where the time goes in v1:
time: 331 us; the launch traced here: 330 us
  waiting for transfers between devices  201 us (61%)
  blocking collectives  56.3 us (17%)
  matrix products  42.3 us (13%)
  between operations  13.8 us (4%)
  local copies, waits for them, and re-layouts  8.21 us (2%)
  other arithmetic  7.47 us (2%)
    all_gather x1, waiting for transfers between devices, shards(): mine = lax.all_gather(mine, 'tp', axis=1, tiled=True)  48.1 us
    reduce_scatter x1, waiting for transfers between devices, shards(): lax.psum_scatter(gate, 'seq', scatter_dimension=0, tiled=True)  47.2 us
    reduce_scatter x1, waiting for transfers between devices, shards(): lax.psum_scatter(partial_sum, 'tp', scatter_dimension=1, tiled=True)  44.2 us
    all_gather x1, waiting for transfers between devices, shards(): hidden = lax.all_gather(hidden, 'seq', axis=0, tiled=True)  35 us
    all_to_all x1, blocking collectives, shards(): lax.all_to_all(mine, 'seq', split_axis=1, concat_axis=0, tiled=True)  28.9 us
    all_to_all x1, blocking collectives, shards(): lax.all_to_all(partial_sum, 'seq', split_axis=0, concat_axis=1, tiled=True)  27.4 us
    reduce_scatter x1, waiting for transfers between devices, shards(): lax.psum_scatter(up, 'seq', scatter_dimension=0, tiled=True)  26.8 us
    dot_general x1, matrix products, shards(): jnp.dot(inputs, gate_weight, preferred_element_type=jnp.float32)  14.4 us
  transfers between devices with their start and end apart: 5, of which 5 were waited for; matrix products, arithmetic and copies ran while one was open for 4% of the time, Pallas kernels for 0%

profile of v1, /device:TPU:1, one launch (start us, length us, event | category | flops | bytes accessed | tf_op | source)
XLA Modules:
  0.0 329.8 jit_solution(6270447324744542222)
XLA Ops:
  7.2 0.0 all-gather.3.cloned.1.call-start
  7.2 1.3 copy.17
  8.5 1.6 fusion.7
  10.1 0.0 all-gather.3.cloned.1.call-update
  10.1 0.0 reduce-scatter.6.cloned.1.call-start
  10.2 48.1 %all-gather.3.cloned.1.call-done = bf16[128,8192]{0,1:T(8,128)(2,1)} async-done(((bf16[128,2048]{0,1:T(8,128)(2,1)}), bf16[128,8192]{0,1:T(8,128)(2,1)}) %all-gather.3.cloned.1.call-update) | async-done | bytes 2097168 | tf_op jit(solution)/shard_map/all_gather | solution.py:21
  58.3 28.9 %all_to_all.38 = bf16[128,4,2048]{0,2,1:T(8,128)(2,1)S(1)} all-to-all(bf16[128,4,2048]{0,2,1:T(8,128)(2,1)} %bitcast.30), channel_id=1, replica_groups=mesh['groups'=2,'tp'=4,'seq'=4] {'seq'}, dimensions={1} | all-to-all | bytes 4194304 | tf_op jit(solution)/shard_map/all_to_all | solution.py:22
  87.2 2.7 copy.18
  90.0 14.3 %convolution_convert_fusion = bf16[512,4096]{1,0:T(8,128)(2,1)} fusion(bf16[512,2048]{1,0:T(8,128)(2,1)} %bitcast.28, bf16[2048,4096]{1,0:T(8,128)(2,1)} %param.8), kind=kOutput, calls=%fused_computation | convolution fusion | flops 8592031744 | bytes 23068672 | tf_op jit(solution)/shard_map/dot_general | solution.py:24
  104.3 0.0 reduce-scatter.6.cloned.1.call-update
  104.3 0.0 reduce-scatter.4.cloned.1.call-start
  104.4 1.5 copy-done
  105.9 14.4 %convolution_convert_fusion.1 = bf16[512,4096]{1,0:T(8,128)(2,1)} fusion(bf16[512,2048]{1,0:T(8,128)(2,1)S(1)} %bitcast.29, bf16[2048,4096]{1,0:T(8,128)(2,1)} %param.7), kind=kOutput, calls=%fused_computation.1 | convolution fusion | flops 8592031744 | bytes 23068672 | tf_op jit(solution)/shard_map/dot_general | solution.py:23
  120.3 0.0 reduce-scatter.4.cloned.1.call-update
  120.3 0.0 all-gather.5.cloned.1.call-start
  120.4 26.8 %reduce-scatter.6.cloned.1.call-done = bf16[128,4096]{1,0:T(8,128)(2,1)} async-done(((bf16[512,4096]{1,0:T(8,128)(2,1)}), bf16[128,4096]{1,0:T(8,128)(2,1)}) %reduce-scatter.6.cloned.1.call-update) | async-done | bytes 1048592 | tf_op jit(solution)/shard_map/reduce_scatter | solution.py:26
  147.2 47.2 %reduce-scatter.4.cloned.1.call-done = bf16[128,4096]{1,0:T(8,128)(2,1)} async-done(((bf16[512,4096]{1,0:T(8,128)(2,1)}), bf16[128,4096]{1,0:T(8,128)(2,1)}) %reduce-scatter.4.cloned.1.call-update) | async-done | bytes 1048592 | tf_op jit(solution)/shard_map/reduce_scatter | solution.py:25
  194.4 3.1 fusion.4
  197.5 0.0 all-gather.5.cloned.1.call-update
  197.5 0.0 reduce-scatter.8.cloned.1.call-start
  197.6 35.0 %all-gather.5.cloned.1.call-done = bf16[512,4096]{1,0:T(8,128)(2,1)} async-done(((bf16[128,4096]{1,0:T(8,128)(2,1)}), bf16[512,4096]{1,0:T(8,128)(2,1)}) %all-gather.5.cloned.1.call-update) | async-done | bytes 4194320 | tf_op jit(solution)/shard_map/all_gather | solution.py:28
  232.6 13.6 %convolution_convert_fusion.2 = bf16[512,2048]{1,0:T(8,128)(2,1)S(1)} fusion(bf16[512,4096]{1,0:T(8,128)(2,1)} %all-gather.5.cloned.1.call-done, bf16[4096,2048]{1,0:T(8,128)(2,1)} %param.9), kind=kOutput, calls=%fused_computation.2 | convolution fusion | flops 8590983168 | bytes 23068672 | tf_op jit(solution)/shard_map/dot_general | solution.py:29
  246.2 27.4 %all_to_all.39 = bf16[4,128,2048]{2,1,0:T(8,128)(2,1)S(1)} all-to-all(bf16[4,128,2048]{2,1,0:T(8,128)(2,1)S(1)} %bitcast.31), channel_id=1, replica_groups=mesh['groups'=2,'tp'=4,'seq'=4] {'seq'}, dimensions={0} | all-to-all | bytes 4194304 | tf_op jit(solution)/shard_map/all_to_all | solution.py:30
  273.6 1.5 copy.21
  275.0 0.0 reduce-scatter.8.cloned.1.call-update
  275.1 44.2 %reduce-scatter.8.cloned.1.call-done = bf16[128,2048]{1,0:T(8,128)(2,1)} async-done(((bf16[128,8192]{1,0:T(8,128)(2,1)}), bf16[128,2048]{1,0:T(8,128)(2,1)}) %reduce-scatter.8.cloned.1.call-update) | async-done | bytes 524304 | tf_op jit(solution)/shard_map/reduce_scatter | solution.py:31
  319.3 1.2 fusion.5
  320.5 0.2 copy.22
  320.7 0.3 reduce_max.9
  321.1 0.7 copy.20
  321.8 0.3 div.16
  322.1 1.2 fusion.6
  (4 shorter events, 0.0 us)
Async XLA Ops:
  7.2 51.2 %all-gather.3.cloned.1.call-start = ((), (), s32[]{:S(2)}) async-start(), calls=%async_computation.5 | async-start | bytes 2621440 | tf_op jit(solution)/shard_map/all_gather | solution.py:21
  10.1 137.0 %reduce-scatter.6.cloned.1.call-start = ((), (), s32[]{:S(2)}) async-start(), calls=%async_computation.7 | async-start | bytes 5242880 | tf_op jit(solution)/shard_map/reduce_scatter | solution.py:26
  104.3 1.6 copy-start
  104.3 90.1 %reduce-scatter.4.cloned.1.call-start = ((), (), s32[]{:S(2)}) async-start(), calls=%async_computation.6 | async-start | bytes 5242880 | tf_op jit(solution)/shard_map/reduce_scatter | solution.py:25
  120.3 112.3 %all-gather.5.cloned.1.call-start = ((), (), s32[]{:S(2)}) async-start(), calls=%async_computation.8 | async-start | bytes 5242880 | tf_op jit(solution)/shard_map/all_gather | solution.py:28
  197.5 121.8 %reduce-scatter.8.cloned.1.call-start = ((), (), s32[]{:S(2)}) async-start(), calls=%async_computation.9 | async-start | bytes 2621440 | tf_op jit(solution)/shard_map/reduce_scatter | solution.py:31
  319.3 2.8 copy-start.1
Sparse Core Ops, SparseCore 0:
  10.3 48.0 all-gather.2
  104.4 42.6 reduce-scatter.5
  149.8 44.4 reduce-scatter.3
  197.7 34.8 all-gather.4
  275.2 44.0 reduce-scatter.7

commit v2 on v1

v2 whole, which is shorter than its diff:
```python
import jax
import jax.numpy as jnp
from jax import lax
from jax.sharding import PartitionSpec as P

CHUNKS = 2


def blocks(array):
    return array.reshape(array.shape[0], array.shape[1] // 128, 128)


def block_scale(array):
    return jnp.max(jnp.abs(blocks(array)), axis=2) + 1e-06


def expand(values, scales):
    return (blocks(values.astype(jnp.float32)) * scales[:, :, None]).reshape(values.shape)


def scaled(total):
    scales = block_scale(total)
    values = (blocks(total) / scales[:, :, None]).reshape(total.shape).astype(jnp.bfloat16)
    return values, scales


def wide(array):
    return array.astype(jnp.float32)


def narrow(array):
    return array.astype(jnp.bfloat16)


def dot(a, b):
    return jnp.dot(a, b, preferred_element_type=jnp.float32)


def any_shards(tokens_values, tokens_scales, gate_weight, up_weight, down_weight):
    mine = narrow(expand(tokens_values, tokens_scales))
    mine = lax.all_gather(mine, "tp", axis=1, tiled=True)
    inputs = lax.all_to_all(mine, "seq", split_axis=1, concat_axis=0, tiled=True)
    gate = narrow(dot(inputs, gate_weight))
    up = narrow(dot(inputs, up_weight))
    gate = wide(lax.psum_scatter(gate, "seq", scatter_dimension=0, tiled=True))
    up = wide(lax.psum_scatter(up, "seq", scatter_dimension=0, tiled=True))
    hidden = narrow(jax.nn.silu(gate) * up)
    hidden = lax.all_gather(hidden, "seq", axis=0, tiled=True)
    partial_sum = narrow(dot(hidden, down_weight))
    partial_sum = lax.all_to_all(partial_sum, "seq", split_axis=0, concat_axis=1, tiled=True)
    return scaled(wide(lax.psum_scatter(partial_sum, "tp", scatter_dimension=1, tiled=True)))


def over_seq(array, bit):
    return lax.ppermute(array, "seq", [(i, i ^ bit) for i in range(4)])


def over_tp(array, bit):
    return lax.ppermute(array, "tp", [(i, i ^ bit) for i in range(4)])


def device(tp, seq):
    return tp * 4 + seq


FIRST_IN, SECOND, FIRST_OUT = [], [], []
for tp in range(4):
    for seq in range(4):
        if (tp ^ seq) & 1:
            FIRST_IN.append((device(tp, seq), device(tp, seq ^ 1)))
            SECOND.append((device(tp, seq), device(tp ^ 1, seq ^ 1)))
            FIRST_OUT.append((device(tp, seq), device(tp ^ 1, seq)))
        else:
            FIRST_IN.append((device(tp, seq), device(tp ^ 1, seq)))
            FIRST_OUT.append((device(tp, seq), device(tp, seq ^ 1)))


def over_both(array, pairs):
    return lax.ppermute(array, ("tp", "seq"), pairs)


def arrange(low_first, one, other):
    return jnp.concatenate([jnp.where(low_first, one, other), jnp.where(low_first, other, one)], axis=0)


def gather_inputs(mine, place):
    tp, seq = place
    x, c, even = seq >> 1, seq & 1, (tp ^ seq) & 1 == 0
    high = tp >> 1
    far = over_tp(mine, 2)
    sent = jnp.where(high == x, far, mine)
    kept = jnp.where(high == x, mine, far)
    got = over_seq(sent, 2)
    pair = arrange(x == 0, kept, got)
    first = over_both(pair, FIRST_IN)
    second = over_both(pair, SECOND)
    own = jnp.where(even, pair, first)
    others = jnp.where(even, first, second)
    return arrange(c == 0, own, others)


def scatter_outputs(partial_sum, place):
    tp, seq = place
    x, c, even = seq >> 1, seq & 1, (tp ^ seq) & 1 == 0
    high = tp >> 1
    half = partial_sum.shape[0] // 2
    rows = half // 2
    low, top = partial_sum[:half], partial_sum[half:]
    own = jnp.where(c == 0, low, top)
    others = jnp.where(c == 0, top, low)
    first = over_both(narrow(jnp.where(even, others, own)), FIRST_OUT)
    second = over_both(narrow(others), SECOND)
    pair = wide(first) + jnp.where(even, own, wide(second))
    low, top = pair[:rows], pair[rows:]
    kept = jnp.where(x == 0, low, top)
    got = over_seq(narrow(jnp.where(x == 0, top, low)), 2)
    sent = jnp.where(high == x, got, narrow(kept))
    held = jnp.where(high == x, kept, wide(got))
    return held + wide(over_tp(sent, 2))


def four_shards(tokens_values, tokens_scales, gate_weight, up_weight, down_weight):
    tp, seq = lax.axis_index("tp"), lax.axis_index("seq")
    place = tp, seq
    width = gate_weight.shape[1] // 4
    rows = tokens_values.shape[0] // CHUNKS

    def columns(weight, bits):
        return lax.dynamic_slice_in_dim(weight, (seq ^ bits) * width, width, axis=1)

    def depth(weight, bits):
        return lax.dynamic_slice_in_dim(weight, (seq ^ bits) * width, width, axis=0)

    mine = narrow(expand(tokens_values, tokens_scales))
    inputs = [gather_inputs(mine[i * rows : (i + 1) * rows], place) for i in range(CHUNKS)]

    def reduced(some, weight):
        a = over_seq(narrow(dot(some, columns(weight, 3))), 1)
        b = over_seq(narrow(dot(some, columns(weight, 2)) + wide(a)), 2)
        c = over_seq(narrow(dot(some, columns(weight, 1))), 1)
        return dot(some, columns(weight, 0)) + wide(c) + wide(b)

    outs = []
    for some in inputs:
        gate = reduced(some, gate_weight)
        up = reduced(some, up_weight)
        hidden = narrow(jax.nn.silu(gate) * up)
        far = over_seq(hidden, 2)
        near = over_seq(hidden, 1)
        last = over_seq(far, 1)
        partial_sum = dot(hidden, depth(down_weight, 0)) + dot(near, depth(down_weight, 1))
        partial_sum += dot(far, depth(down_weight, 2))
        partial_sum += dot(last, depth(down_weight, 3))
        outs.append(scaled(scatter_outputs(partial_sum, place)))
    return tuple(jnp.concatenate(parts, axis=0) for parts in zip(*outs))


def solution(mesh):
    placed = (
        P(("groups", "seq"), "tp"),
        P(("groups", "seq"), "tp"),
        P("seq", "tp"),
        P("seq", "tp"),
        P("tp", "seq"),
    )
    fours = mesh.shape["tp"] == 4 and mesh.shape["seq"] == 4
    return jax.shard_map(
        four_shards if fours else any_shards,
        mesh=mesh,
        in_specs=placed,
        out_specs=(P(("groups", "seq"), "tp"), P(("groups", "seq"), "tp")),
        check_vma=False,
    )
```

time: 331 us -> 208 us (0.63)
  waiting for transfers between devices: 201 us -> 98.3 us
  blocking collectives: 56.3 us -> 0 us
  starting transfers between devices: 0.21 us -> 44.8 us
  between operations: 13.8 us -> 1.3 us
  matrix products: 42.3 us -> 54.2 us
  local copies, waits for them, and re-layouts: 8.21 us -> 1.9 us
    reduce_scatter x3 -> x0, waiting for transfers between devices: 118 us -> none  [the longest x1 47.2 us: shards(): lax.psum_scatter(gate, 'seq', scatter_dimension=0, tiled=True)]
    ppermute x0 -> x34, waiting for transfers between devices: none -> 98.3 us  [the longest x4 37.1 us: over_tp(): return lax.ppermute(array, 'tp', [(i, i ^ bit) for i in range(4)])]
    all_gather x2 -> x0, waiting for transfers between devices: 83.1 us -> none  [the longest x1 48.1 us: shards(): mine = lax.all_gather(mine, 'tp', axis=1, tiled=True)]
    all_to_all x2 -> x0, blocking collectives: 56.3 us -> none  [the longest x1 28.9 us: shards(): lax.all_to_all(mine, 'seq', split_axis=1, concat_axis=0, tiled=True)]
    ppermute x0 -> x34, starting transfers between devices: none -> 44.8 us  [the longest x8 18.1 us: over_both(): return lax.ppermute(array, ('tp', 'seq'), pairs)]
    dot_general x3 -> x24, matrix products: 42.3 us -> 54.2 us  [dot(): return jnp.dot(a, b, preferred_element_type=jnp.float32)]
    all_to_all x2 -> x0, local copies, waits for them, and re-layouts: 4.2 us -> none  [the longest x1 2.72 us: shards(): lax.all_to_all(mine, 'seq', split_axis=1, concat_axis=0, tiled=True)]
    convert_element_type x3 -> x7, other arithmetic: 5.9 us -> 2.23 us  [the longest x5 1.71 us: narrow(): return array.astype(jnp.bfloat16)]
  transfers between devices with their start and end apart: 5 -> 34, of which waited for: 5 -> 16; matrix products, arithmetic and copies ran while one was open for 4% -> 28% of each run, Pallas kernels for 0% -> 0%
where the time goes in v2:
time: 208 us; the launch traced here: 206 us
  waiting for transfers between devices  98.3 us (47%)
  matrix products  54.2 us (26%)
  starting transfers between devices  44.8 us (22%)
  other arithmetic  5.91 us (3%)
    dot_general x24, matrix products, dot(): return jnp.dot(a, b, preferred_element_type=jnp.float32)  54.2 us
    ppermute x4, waiting for transfers between devices, over_tp(): return lax.ppermute(array, 'tp', [(i, i ^ bit) for i in range(4)])  37.1 us
    ppermute x22, waiting for transfers between devices, over_seq(): return lax.ppermute(array, 'seq', [(i, i ^ bit) for i in range(4)])  34.1 us
    ppermute x8, waiting for transfers between devices, over_both(): return lax.ppermute(array, ('tp', 'seq'), pairs)  27 us
    ppermute x8, starting transfers between devices, over_both(): return lax.ppermute(array, ('tp', 'seq'), pairs)  18.1 us
    ppermute x22, starting transfers between devices, over_seq(): return lax.ppermute(array, 'seq', [(i, i ^ bit) for i in range(4)])  17.3 us
    ppermute x4, starting transfers between devices, over_tp(): return lax.ppermute(array, 'tp', [(i, i ^ bit) for i in range(4)])  9.4 us
  transfers between devices with their start and end apart: 34, of which 16 were waited for; matrix products, arithmetic and copies ran while one was open for 28% of the time, Pallas kernels for 0%

profile of v2, /device:TPU:1, one launch (start us, length us, event | category | flops | bytes accessed | tf_op | source)
XLA Modules:
  0.0 206.4 jit_solution(8786150377574186854)
XLA Ops:
  3.2 3.2 %collective-permute-start = (bf16[64,2048]{1,0:T(8,128)(2,1)S(1)}, bf16[64,2048]{1,0:T(8,128)(2,1)S(1)}, u32[]{:S(2)}, u32[]{:S(2)}) collective-permute-start(bf16[64,2048]{1,0:T(8,128)(2,1)S(1)} %slice.40), channel_id=1, source_target_pairs={{0,8},{4,12},{8,0},{12,4},{1,9},{5,13},{9,1},{13,5},{2,10},{6,14},... | collective-permute-start | bytes 786440 | tf_op jit(solution)/shard_map/ppermute | solution.py:59
  6.4 11.6 %collective-permute-done = bf16[64,2048]{1,0:T(8,128)(2,1)S(1)} collective-permute-done((bf16[64,2048]{1,0:T(8,128)(2,1)S(1)}, bf16[64,2048]{1,0:T(8,128)(2,1)S(1)}, u32[]{:S(2)}, u32[]{:S(2)}) %collective-permute-start) | collective-permute-done | bytes 262176 | tf_op jit(solution)/shard_map/ppermute | solution.py:59
  19.1 5.6 %collective-permute-done.1 = bf16[64,2048]{1,0:T(8,128)(2,1)S(1)} collective-permute-done((bf16[64,2048]{1,0:T(8,128)(2,1)S(1)}, bf16[64,2048]{1,0:T(8,128)(2,1)S(1)}, u32[]{:S(2)}, u32[]{:S(2)}) %collective-permute-start.1) | collective-permute-done | bytes 262176 | tf_op jit(solution)/shard_map/ppermute | solution.py:55
  24.8 12.2 %collective-permute-done.17 = bf16[64,2048]{1,0:T(8,128)(2,1)S(1)} collective-permute-done((bf16[64,2048]{1,0:T(8,128)(2,1)S(1)}, bf16[64,2048]{1,0:T(8,128)(2,1)S(1)}, u32[]{:S(2)}, u32[]{:S(2)}) %collective-permute-start.17) | collective-permute-done | bytes 262176 | tf_op jit(solution)/shard_map/ppermute | solution.py:59
  37.2 4.1 %collective-permute-start.2 = (bf16[128,2048]{1,0:T(8,128)(2,1)S(1)}, bf16[128,2048]{1,0:T(8,128)(2,1)S(1)}, u32[]{:S(2)}, u32[]{:S(2)}) collective-permute-start(bf16[128,2048]{1,0:T(8,128)(2,1)S(1)} %pad_maximum_fusion.2), channel_id=1, source_target_pairs={{0,4},{1,0},{2,6},{3,2},{4,5},{5,1},{6,7},{7,3},{8,12},{9,8},{10,1... | collective-permute-start | bytes 1572872 | tf_op jit(solution)/shard_map/ppermute | solution.py:79
  41.3 1.9 collective-permute-start.3
  43.4 3.4 %collective-permute-start.19 = (bf16[128,2048]{1,0:T(8,128)(2,1)S(1)}, bf16[128,2048]{1,0:T(8,128)(2,1)S(1)}, u32[]{:S(2)}, u32[]{:S(2)}) collective-permute-start(bf16[128,2048]{1,0:T(8,128)(2,1)S(1)} %pad_maximum_fusion.3), channel_id=1, source_target_pairs={{0,4},{1,0},{2,6},{3,2},{4,5},{5,1},{6,7},{7,3},{8,12},{9,8},{10,1... | collective-permute-start | bytes 1572872 | tf_op jit(solution)/shard_map/ppermute | solution.py:79
  48.6 8.7 %collective-permute-done.3 = bf16[128,2048]{1,0:T(8,128)(2,1)S(1)} collective-permute-done((bf16[128,2048]{1,0:T(8,128)(2,1)S(1)}, bf16[128,2048]{1,0:T(8,128)(2,1)S(1)}, u32[]{:S(2)}, u32[]{:S(2)}) %collective-permute-start.3) | collective-permute-done | bytes 524320 | tf_op jit(solution)/shard_map/ppermute | solution.py:79
  57.7 3.6 %fusion.120 = bf16[256,1024]{1,0:T(8,128)(2,1)S(1)} fusion(bf16[2048,4096]{1,0:T(8,128)(2,1)} %param.7, s32[]{:T(128)S(6)} %select_n.191, bf16[128,2048]{1,0:T(8,128)(2,1)S(1)} %get-tuple-element.13, bf16[128,2048]{1,0:T(8,128)(2,1)S(1)} %get-tuple-element.12), kind=kOutput, calls=%fused_computation.72 | convolution fusion | flops 1076101120 | bytes 5767172 | tf_op jit(solution)/shard_map/dot_general | solution.py:36
  61.4 3.6 %fusion.114 = bf16[256,1024]{1,0:T(8,128)(2,1)S(1)} fusion(bf16[2048,4096]{1,0:T(8,128)(2,1)} %param.7, s32[]{:T(128)S(6)} %select_n.189, bf16[128,2048]{1,0:T(8,128)(2,1)S(1)} %get-tuple-element.13, bf16[128,2048]{1,0:T(8,128)(2,1)S(1)} %get-tuple-element.12), kind=kOutput, calls=%fused_computation.70 | convolution fusion | flops 1076101120 | bytes 5767172 | tf_op jit(solution)/shard_map/dot_general | solution.py:36
  65.4 3.7 %fusion.132 = bf16[256,1024]{1,0:T(8,128)(2,1)S(1)} fusion(bf16[2048,4096]{1,0:T(8,128)(2,1)} %param.8, s32[]{:T(128)S(6)} %select_n.191, bf16[128,2048]{1,0:T(8,128)(2,1)S(1)} %get-tuple-element.13, bf16[128,2048]{1,0:T(8,128)(2,1)S(1)} %get-tuple-element.12), kind=kOutput, calls=%fused_computation.76 | convolution fusion | flops 1076101120 | bytes 5767172 | tf_op jit(solution)/shard_map/dot_general | solution.py:36
  69.3 3.6 %fusion.126 = bf16[256,1024]{1,0:T(8,128)(2,1)S(1)} fusion(bf16[2048,4096]{1,0:T(8,128)(2,1)} %param.8, s32[]{:T(128)S(6)} %select_n.189, bf16[128,2048]{1,0:T(8,128)(2,1)S(1)} %get-tuple-element.13, bf16[128,2048]{1,0:T(8,128)(2,1)S(1)} %get-tuple-element.12), kind=kOutput, calls=%fused_computation.74 | convolution fusion | flops 1076101120 | bytes 5767172 | tf_op jit(solution)/shard_map/dot_general | solution.py:36
  78.5 3.5 %fusion.135 = bf16[256,1024]{1,0:T(8,128)(2,1)S(1)} fusion(bf16[2048,4096]{1,0:T(8,128)(2,1)} %param.8, s32[]{:T(128)S(6)} %select_n.191, bf16[128,2048]{1,0:T(8,128)(2,1)S(1)} %get-tuple-element.15, bf16[128,2048]{1,0:T(8,128)(2,1)S(1)} %get-tuple-element.14), kind=kOutput, calls=%fused_computation.77 | convolution fusion | flops 1076101120 | bytes 5767172 | tf_op jit(solution)/shard_map/dot_general | solution.py:36
  82.5 3.5 %fusion.105 = bf16[256,1024]{1,0:T(8,128)(2,1)S(1)} fusion(bf16[2048,4096]{1,0:T(8,128)(2,1)} %param.8, s32[]{:T(128)S(6)} %select_n.190, bf16[256,1024]{1,0:T(8,128)(2,1)S(1)} %collective-permute-done.8, bf16[128,2048]{1,0:T(8,128)(2,1)S(1)} %get-tuple-element.13, bf16[128,2048]{1,0:T(8,128)(2,1)S(1)} %get-tuple-element.12), kind=kOutput, calls=%fused_computation.67 | convolution fusion | flops 1076625408 | bytes 6291460 | tf_op jit(solution)/shard_map/dot_general | solution.py:36
  86.0 3.5 %fusion.129 = bf16[256,1024]{1,0:T(8,128)(2,1)S(1)} fusion(bf16[2048,4096]{1,0:T(8,128)(2,1)} %param.8, s32[]{:T(128)S(6)} %select_n.189, bf16[128,2048]{1,0:T(8,128)(2,1)S(1)} %get-tuple-element.15, bf16[128,2048]{1,0:T(8,128)(2,1)S(1)} %get-tuple-element.14), kind=kOutput, calls=%fused_computation.75 | convolution fusion | flops 1076101120 | bytes 5767172 | tf_op jit(solution)/shard_map/dot_general | solution.py:36
  94.5 3.5 %fusion.102 = bf16[256,1024]{1,0:T(8,128)(2,1)S(1)} fusion(bf16[2048,4096]{1,0:T(8,128)(2,1)} %param.8, s32[]{:T(128)S(6)} %select_n.190, bf16[256,1024]{1,0:T(8,128)(2,1)S(1)} %collective-permute-done.25, bf16[128,2048]{1,0:T(8,128)(2,1)S(1)} %get-tuple-element.15, bf16[128,2048]{1,0:T(8,128)(2,1)S(1)} %get-tuple-element.14), kind=kOutput, calls=%fused_computation.66 | convolution fusion | flops 1076625408 | bytes 6291460 | tf_op jit(solution)/shard_map/dot_general | solution.py:36
  98.8 5.8 %collective-permute-done.9 = bf16[256,1024]{1,0:T(8,128)(2,1)S(1)} collective-permute-done((bf16[256,1024]{1,0:T(8,128)(2,1)S(1)}, bf16[256,1024]{1,0:T(8,128)(2,1)S(1)}, u32[]{:S(2)}, u32[]{:S(2)}) %collective-permute-start.9) | collective-permute-done | bytes 524320 | tf_op jit(solution)/shard_map/ppermute | solution.py:55
  104.6 3.8 %multiply_convert_fusion.1 = bf16[256,1024]{1,0:T(8,128)(2,1)S(1)} fusion(f32[256,1024]{1,0:T(8,128)S(1)} %fusion.69, bf16[256,1024]{1,0:T(8,128)(2,1)S(1)} %collective-permute-done.9, bf16[256,1024]{1,0:T(8,128)(2,1)S(1)} %collective-permute-done.7, bf16[2048,4096]{1,0:T(8,128)(2,1)} %param.8, s32[]{:T(128)S(6)} %select_n.188, ...), kind=kOutput, calls=%fused_computation.87 | convolution fusion | flops 1078460416 | bytes 7864324 | tf_op jit(solution)/shard_map/dot_general | solution.py:36
  109.4 2.2 %collective-permute-start.10 = (bf16[256,1024]{1,0:T(8,128)(2,1)S(1)}, bf16[256,1024]{1,0:T(8,128)(2,1)S(1)}, u32[]{:S(2)}, u32[]{:S(2)}) collective-permute-start(bf16[256,1024]{1,0:T(8,128)(2,1)S(1)} %multiply_convert_fusion.1), channel_id=1, source_target_pairs={{0,1},{1,0},{2,3},{3,2},{4,5},{5,4},{6,7},{7,6},{8,9},{9,8},{10,11... | collective-permute-start | bytes 1572872 | tf_op jit(solution)/shard_map/ppermute | solution.py:55
  111.5 4.3 %collective-permute-done.23 = bf16[256,1024]{1,0:T(8,128)(2,1)S(1)} collective-permute-done((bf16[256,1024]{1,0:T(8,128)(2,1)S(1)}, bf16[256,1024]{1,0:T(8,128)(2,1)S(1)}, u32[]{:S(2)}, u32[]{:S(2)}) %collective-permute-start.23) | collective-permute-done | bytes 524320 | tf_op jit(solution)/shard_map/ppermute | solution.py:55
  117.2 9.9 %collective-permute-done.26 = bf16[256,1024]{1,0:T(8,128)(2,1)S(1)} collective-permute-done((bf16[256,1024]{1,0:T(8,128)(2,1)S(1)}, bf16[256,1024]{1,0:T(8,128)(2,1)S(1)}, u32[]{:S(2)}, u32[]{:S(2)}) %collective-permute-start.26) | collective-permute-done | bytes 524320 | tf_op jit(solution)/shard_map/ppermute | solution.py:55
  127.1 3.7 %multiply_convert_fusion = bf16[256,1024]{1,0:T(8,128)(2,1)S(1)} fusion(f32[256,1024]{1,0:T(8,128)S(1)} %fusion.75, bf16[256,1024]{1,0:T(8,128)(2,1)S(1)} %collective-permute-done.26, bf16[256,1024]{1,0:T(8,128)(2,1)S(1)} %collective-permute-done.24, bf16[2048,4096]{1,0:T(8,128)(2,1)} %param.8, s32[]{:T(128)S(6)} %select_n.188, ...), kind=kOutput, calls=%fused_computation.84 | convolution fusion | flops 1078460416 | bytes 7864324 | tf_op jit(solution)/shard_map/dot_general | solution.py:36
  131.7 2.2 %collective-permute-start.27 = (bf16[256,1024]{1,0:T(8,128)(2,1)S(1)}, bf16[256,1024]{1,0:T(8,128)(2,1)S(1)}, u32[]{:S(2)}, u32[]{:S(2)}) collective-permute-start(bf16[256,1024]{1,0:T(8,128)(2,1)S(1)} %multiply_convert_fusion), channel_id=1, source_target_pairs={{0,1},{1,0},{2,3},{3,2},{4,5},{5,4},{6,7},{7,6},{8,9},{9,8},{10,11... | collective-permute-start | bytes 1572872 | tf_op jit(solution)/shard_map/ppermute | solution.py:55
  133.8 4.5 %collective-permute-done.11 = bf16[256,1024]{1,0:T(8,128)(2,1)S(1)} collective-permute-done((bf16[256,1024]{1,0:T(8,128)(2,1)S(1)}, bf16[256,1024]{1,0:T(8,128)(2,1)S(1)}, u32[]{:S(2)}, u32[]{:S(2)}) %collective-permute-start.11) | collective-permute-done | bytes 524320 | tf_op jit(solution)/shard_map/ppermute | solution.py:55
  145.6 2.1 %collective-permute-start.14 = (bf16[128,2048]{1,0:T(8,128)(2,1)S(1)}, bf16[128,2048]{1,0:T(8,128)(2,1)S(1)}, u32[]{:S(2)}, u32[]{:S(2)}) collective-permute-start(bf16[128,2048]{1,0:T(8,128)(2,1)S(1)} %get-tuple-element.9), channel_id=1, source_target_pairs={{1,4},{3,6},{4,1},{6,3},{9,12},{11,14},{12,9},{14,11},{17,20},{19,... | collective-permute-start | bytes 1572872 | tf_op jit(solution)/shard_map/ppermute | solution.py:79
  156.1 3.3 %collective-permute-done.13 = bf16[128,2048]{1,0:T(8,128)(2,1)S(1)} collective-permute-done((bf16[128,2048]{1,0:T(8,128)(2,1)S(1)}, bf16[128,2048]{1,0:T(8,128)(2,1)S(1)}, u32[]{:S(2)}, u32[]{:S(2)}) %collective-permute-start.13) | collective-permute-done | bytes 524320 | tf_op jit(solution)/shard_map/ppermute | solution.py:79
  162.0 4.3 %collective-permute-start.31 = (bf16[128,2048]{1,0:T(8,128)(2,1)S(1)}, bf16[128,2048]{1,0:T(8,128)(2,1)S(1)}, u32[]{:S(2)}, u32[]{:S(2)}) collective-permute-start(bf16[128,2048]{1,0:T(8,128)(2,1)S(1)} %get-tuple-element.11), channel_id=1, source_target_pairs={{1,4},{3,6},{4,1},{6,3},{9,12},{11,14},{12,9},{14,11},{17,20},{19,... | collective-permute-start | bytes 1572872 | tf_op jit(solution)/shard_map/ppermute | solution.py:79
  167.4 11.4 %collective-permute-done.31 = bf16[128,2048]{1,0:T(8,128)(2,1)S(1)} collective-permute-done((bf16[128,2048]{1,0:T(8,128)(2,1)S(1)}, bf16[128,2048]{1,0:T(8,128)(2,1)S(1)}, u32[]{:S(2)}, u32[]{:S(2)}) %collective-permute-start.31) | collective-permute-done | bytes 524320 | tf_op jit(solution)/shard_map/ppermute | solution.py:79
  178.9 2.1 collective-permute-done.30
  184.2 2.3 %collective-permute-done.32 = bf16[64,2048]{1,0:T(8,128)(2,1)S(1)} collective-permute-done((bf16[64,2048]{1,0:T(8,128)(2,1)S(1)}, bf16[64,2048]{1,0:T(8,128)(2,1)S(1)}, u32[]{:S(2)}, u32[]{:S(2)}) %collective-permute-start.32) | collective-permute-done | bytes 262176 | tf_op jit(solution)/shard_map/ppermute | solution.py:55
  186.7 5.3 %collective-permute-start.33 = (bf16[64,2048]{1,0:T(8,128)(2,1)S(1)}, bf16[64,2048]{1,0:T(8,128)(2,1)S(1)}, u32[]{:S(2)}, u32[]{:S(2)}) collective-permute-start(bf16[64,2048]{1,0:T(8,128)(2,1)S(1)} %get-tuple-element.6), channel_id=1, source_target_pairs={{0,8},{4,12},{8,0},{12,4},{1,9},{5,13},{9,1},{13,5},{2,10},{6,14},... | collective-permute-start | bytes 786440 | tf_op jit(solution)/shard_map/ppermute | solution.py:59
  192.4 11.5 %collective-permute-done.33 = bf16[64,2048]{1,0:T(8,128)(2,1)S(1)} collective-permute-done((bf16[64,2048]{1,0:T(8,128)(2,1)S(1)}, bf16[64,2048]{1,0:T(8,128)(2,1)S(1)}, u32[]{:S(2)}, u32[]{:S(2)}) %collective-permute-start.33) | collective-permute-done | bytes 262176 | tf_op jit(solution)/shard_map/ppermute | solution.py:59
  (114 shorter events, 47.1 us)
Async XLA Ops:
  3.2 14.9 %collective-permute-start = (bf16[64,2048]{1,0:T(8,128)(2,1)S(1)}, bf16[64,2048]{1,0:T(8,128)(2,1)S(1)}, u32[]{:S(2)}, u32[]{:S(2)}) collective-permute-start(bf16[64,2048]{1,0:T(8,128)(2,1)S(1)} %slice.40), channel_id=1, source_target_pairs={{0,8},{4,12},{8,0},{12,4},{1,9},{5,13},{9,1},{13,5},{2,10},{6,14},... | collective-permute-start | bytes 786440 | tf_op jit(solution)/shard_map/ppermute | solution.py:59
  18.1 6.6 %collective-permute-start.1 = (bf16[64,2048]{1,0:T(8,128)(2,1)S(1)}, bf16[64,2048]{1,0:T(8,128)(2,1)S(1)}, u32[]{:S(2)}, u32[]{:S(2)}) collective-permute-start(bf16[64,2048]{1,0:T(8,128)(2,1)S(1)} %broadcast_select_fusion.14), channel_id=1, source_target_pairs={{0,2},{1,3},{2,0},{3,1},{4,6},{5,7},{6,4},{7,5},{8,10},{9,11},{10,... | collective-permute-start | bytes 786440 | tf_op jit(solution)/shard_map/ppermute | solution.py:55
  24.8 12.3 %collective-permute-start.17 = (bf16[64,2048]{1,0:T(8,128)(2,1)S(1)}, bf16[64,2048]{1,0:T(8,128)(2,1)S(1)}, u32[]{:S(2)}, u32[]{:S(2)}) collective-permute-start(bf16[64,2048]{1,0:T(8,128)(2,1)S(1)} %get-tuple-element.20), channel_id=1, source_target_pairs={{0,8},{4,12},{8,0},{12,4},{1,9},{5,13},{9,1},{13,5},{2,10},{6,14},... | collective-permute-start | bytes 786440 | tf_op jit(solution)/shard_map/ppermute | solution.py:59
  37.1 6.1 %collective-permute-start.18 = (bf16[64,2048]{1,0:T(8,128)(2,1)S(1)}, bf16[64,2048]{1,0:T(8,128)(2,1)S(1)}, u32[]{:S(2)}, u32[]{:S(2)}) collective-permute-start(bf16[64,2048]{1,0:T(8,128)(2,1)S(1)} %broadcast_select_fusion.12), channel_id=1, source_target_pairs={{0,2},{1,3},{2,0},{3,1},{4,6},{5,7},{6,4},{7,5},{8,10},{9,11},{10,... | collective-permute-start | bytes 786440 | tf_op jit(solution)/shard_map/ppermute | solution.py:55
  37.2 11.4 %collective-permute-start.2 = (bf16[128,2048]{1,0:T(8,128)(2,1)S(1)}, bf16[128,2048]{1,0:T(8,128)(2,1)S(1)}, u32[]{:S(2)}, u32[]{:S(2)}) collective-permute-start(bf16[128,2048]{1,0:T(8,128)(2,1)S(1)} %pad_maximum_fusion.2), channel_id=1, source_target_pairs={{0,4},{1,0},{2,6},{3,2},{4,5},{5,1},{6,7},{7,3},{8,12},{9,8},{10,1... | collective-permute-start | bytes 1572872 | tf_op jit(solution)/shard_map/ppermute | solution.py:79
  41.3 16.0 %collective-permute-start.3 = (bf16[128,2048]{1,0:T(8,128)(2,1)S(1)}, bf16[128,2048]{1,0:T(8,128)(2,1)S(1)}, u32[]{:S(2)}, u32[]{:S(2)}) collective-permute-start(bf16[128,2048]{1,0:T(8,128)(2,1)S(1)} %pad_maximum_fusion.2), channel_id=1, source_target_pairs={{1,4},{3,6},{4,1},{6,3},{9,12},{11,14},{12,9},{14,11},{17,20},{19,... | collective-permute-start | bytes 1572872 | tf_op jit(solution)/shard_map/ppermute | solution.py:79
  43.4 31.5 %collective-permute-start.19 = (bf16[128,2048]{1,0:T(8,128)(2,1)S(1)}, bf16[128,2048]{1,0:T(8,128)(2,1)S(1)}, u32[]{:S(2)}, u32[]{:S(2)}) collective-permute-start(bf16[128,2048]{1,0:T(8,128)(2,1)S(1)} %pad_maximum_fusion.3), channel_id=1, source_target_pairs={{0,4},{1,0},{2,6},{3,2},{4,5},{5,1},{6,7},{7,3},{8,12},{9,8},{10,1... | collective-permute-start | bytes 1572872 | tf_op jit(solution)/shard_map/ppermute | solution.py:79
  46.7 28.8 %collective-permute-start.20 = (bf16[128,2048]{1,0:T(8,128)(2,1)S(1)}, bf16[128,2048]{1,0:T(8,128)(2,1)S(1)}, u32[]{:S(2)}, u32[]{:S(2)}) collective-permute-start(bf16[128,2048]{1,0:T(8,128)(2,1)S(1)} %pad_maximum_fusion.3), channel_id=1, source_target_pairs={{1,4},{3,6},{4,1},{6,3},{9,12},{11,14},{12,9},{14,11},{17,20},{19,... | collective-permute-start | bytes 1572872 | tf_op jit(solution)/shard_map/ppermute | solution.py:79
  61.3 11.6 %collective-permute-start.5 = (bf16[256,1024]{1,0:T(8,128)(2,1)S(1)}, bf16[256,1024]{1,0:T(8,128)(2,1)S(1)}, u32[]{:S(2)}, u32[]{:S(2)}) collective-permute-start(bf16[256,1024]{1,0:T(8,128)(2,1)S(1)} %fusion.120), channel_id=1, source_target_pairs={{0,1},{1,0},{2,3},{3,2},{4,5},{5,4},{6,7},{7,6},{8,9},{9,8},{10,11... | collective-permute-start | bytes 1572872 | tf_op jit(solution)/shard_map/ppermute | solution.py:55
  65.0 24.4 %collective-permute-start.4 = (bf16[256,1024]{1,0:T(8,128)(2,1)S(1)}, bf16[256,1024]{1,0:T(8,128)(2,1)S(1)}, u32[]{:S(2)}, u32[]{:S(2)}) collective-permute-start(bf16[256,1024]{1,0:T(8,128)(2,1)S(1)} %fusion.114), channel_id=1, source_target_pairs={{0,1},{1,0},{2,3},{3,2},{4,5},{5,4},{6,7},{7,6},{8,9},{9,8},{10,11... | collective-permute-start | bytes 1572872 | tf_op jit(solution)/shard_map/ppermute | solution.py:55
  69.1 13.2 %collective-permute-start.8 = (bf16[256,1024]{1,0:T(8,128)(2,1)S(1)}, bf16[256,1024]{1,0:T(8,128)(2,1)S(1)}, u32[]{:S(2)}, u32[]{:S(2)}) collective-permute-start(bf16[256,1024]{1,0:T(8,128)(2,1)S(1)} %fusion.132), channel_id=1, source_target_pairs={{0,1},{1,0},{2,3},{3,2},{4,5},{5,4},{6,7},{7,6},{8,9},{9,8},{10,11... | collective-permute-start | bytes 1572872 | tf_op jit(solution)/shard_map/ppermute | solution.py:55
  72.9 25.0 %collective-permute-start.7 = (bf16[256,1024]{1,0:T(8,128)(2,1)S(1)}, bf16[256,1024]{1,0:T(8,128)(2,1)S(1)}, u32[]{:S(2)}, u32[]{:S(2)}) collective-permute-start(bf16[256,1024]{1,0:T(8,128)(2,1)S(1)} %fusion.126), channel_id=1, source_target_pairs={{0,1},{1,0},{2,3},{3,2},{4,5},{5,4},{6,7},{7,6},{8,9},{9,8},{10,11... | collective-permute-start | bytes 1572872 | tf_op jit(solution)/shard_map/ppermute | solution.py:55
  74.8 15.1 %collective-permute-start.6 = (bf16[256,1024]{1,0:T(8,128)(2,1)S(1)}, bf16[256,1024]{1,0:T(8,128)(2,1)S(1)}, u32[]{:S(2)}, u32[]{:S(2)}) collective-permute-start(bf16[256,1024]{1,0:T(8,128)(2,1)S(1)} %fusion.111), channel_id=1, source_target_pairs={{0,2},{1,3},{2,0},{3,1},{4,6},{5,7},{6,4},{7,5},{8,10},{9,11},{10,... | collective-permute-start | bytes 1572872 | tf_op jit(solution)/shard_map/ppermute | solution.py:55
  81.9 9.4 %collective-permute-start.22 = (bf16[256,1024]{1,0:T(8,128)(2,1)S(1)}, bf16[256,1024]{1,0:T(8,128)(2,1)S(1)}, u32[]{:S(2)}, u32[]{:S(2)}) collective-permute-start(bf16[256,1024]{1,0:T(8,128)(2,1)S(1)} %fusion.123), channel_id=1, source_target_pairs={{0,1},{1,0},{2,3},{3,2},{4,5},{5,4},{6,7},{7,6},{8,9},{9,8},{10,11... | collective-permute-start | bytes 1572872 | tf_op jit(solution)/shard_map/ppermute | solution.py:55
  82.3 27.0 %collective-permute-start.21 = (bf16[256,1024]{1,0:T(8,128)(2,1)S(1)}, bf16[256,1024]{1,0:T(8,128)(2,1)S(1)}, u32[]{:S(2)}, u32[]{:S(2)}) collective-permute-start(bf16[256,1024]{1,0:T(8,128)(2,1)S(1)} %fusion.117), channel_id=1, source_target_pairs={{0,1},{1,0},{2,3},{3,2},{4,5},{5,4},{6,7},{7,6},{8,9},{9,8},{10,11... | collective-permute-start | bytes 1572872 | tf_op jit(solution)/shard_map/ppermute | solution.py:55
  89.9 27.3 %collective-permute-start.24 = (bf16[256,1024]{1,0:T(8,128)(2,1)S(1)}, bf16[256,1024]{1,0:T(8,128)(2,1)S(1)}, u32[]{:S(2)}, u32[]{:S(2)}) collective-permute-start(bf16[256,1024]{1,0:T(8,128)(2,1)S(1)} %fusion.129), channel_id=1, source_target_pairs={{0,1},{1,0},{2,3},{3,2},{4,5},{5,4},{6,7},{7,6},{8,9},{9,8},{10,11... | collective-permute-start | bytes 1572872 | tf_op jit(solution)/shard_map/ppermute | solution.py:55
  91.4 13.3 %collective-permute-start.9 = (bf16[256,1024]{1,0:T(8,128)(2,1)S(1)}, bf16[256,1024]{1,0:T(8,128)(2,1)S(1)}, u32[]{:S(2)}, u32[]{:S(2)}) collective-permute-start(bf16[256,1024]{1,0:T(8,128)(2,1)S(1)} %fusion.105), channel_id=1, source_target_pairs={{0,2},{1,3},{2,0},{3,1},{4,6},{5,7},{6,4},{7,5},{8,10},{9,11},{10,... | collective-permute-start | bytes 1572872 | tf_op jit(solution)/shard_map/ppermute | solution.py:55
  93.7 22.1 %collective-permute-start.23 = (bf16[256,1024]{1,0:T(8,128)(2,1)S(1)}, bf16[256,1024]{1,0:T(8,128)(2,1)S(1)}, u32[]{:S(2)}, u32[]{:S(2)}) collective-permute-start(bf16[256,1024]{1,0:T(8,128)(2,1)S(1)} %fusion.108), channel_id=1, source_target_pairs={{0,2},{1,3},{2,0},{3,1},{4,6},{5,7},{6,4},{7,5},{8,10},{9,11},{10,... | collective-permute-start | bytes 1572872 | tf_op jit(solution)/shard_map/ppermute | solution.py:55
  98.0 29.1 %collective-permute-start.26 = (bf16[256,1024]{1,0:T(8,128)(2,1)S(1)}, bf16[256,1024]{1,0:T(8,128)(2,1)S(1)}, u32[]{:S(2)}, u32[]{:S(2)}) collective-permute-start(bf16[256,1024]{1,0:T(8,128)(2,1)S(1)} %fusion.102), channel_id=1, source_target_pairs={{0,2},{1,3},{2,0},{3,1},{4,6},{5,7},{6,4},{7,5},{8,10},{9,11},{10,... | collective-permute-start | bytes 1572872 | tf_op jit(solution)/shard_map/ppermute | solution.py:55
  108.5 29.9 %collective-permute-start.11 = (bf16[256,1024]{1,0:T(8,128)(2,1)S(1)}, bf16[256,1024]{1,0:T(8,128)(2,1)S(1)}, u32[]{:S(2)}, u32[]{:S(2)}) collective-permute-start(bf16[256,1024]{1,0:T(8,128)(2,1)S(1)} %multiply_convert_fusion.1), channel_id=1, source_target_pairs={{0,2},{1,3},{2,0},{3,1},{4,6},{5,7},{6,4},{7,5},{8,10},{9,11},{10,... | collective-permute-start | bytes 1572872 | tf_op jit(solution)/shard_map/ppermute | solution.py:55
  109.4 32.2 %collective-permute-start.10 = (bf16[256,1024]{1,0:T(8,128)(2,1)S(1)}, bf16[256,1024]{1,0:T(8,128)(2,1)S(1)}, u32[]{:S(2)}, u32[]{:S(2)}) collective-permute-start(bf16[256,1024]{1,0:T(8,128)(2,1)S(1)} %multiply_convert_fusion.1), channel_id=1, source_target_pairs={{0,1},{1,0},{2,3},{3,2},{4,5},{5,4},{6,7},{7,6},{8,9},{9,8},{10,11... | collective-permute-start | bytes 1572872 | tf_op jit(solution)/shard_map/ppermute | solution.py:55
  130.8 18.8 %collective-permute-start.28 = (bf16[256,1024]{1,0:T(8,128)(2,1)S(1)}, bf16[256,1024]{1,0:T(8,128)(2,1)S(1)}, u32[]{:S(2)}, u32[]{:S(2)}) collective-permute-start(bf16[256,1024]{1,0:T(8,128)(2,1)S(1)} %multiply_convert_fusion), channel_id=1, source_target_pairs={{0,2},{1,3},{2,0},{3,1},{4,6},{5,7},{6,4},{7,5},{8,10},{9,11},{10,... | collective-permute-start | bytes 1572872 | tf_op jit(solution)/shard_map/ppermute | solution.py:55
  131.7 20.3 %collective-permute-start.27 = (bf16[256,1024]{1,0:T(8,128)(2,1)S(1)}, bf16[256,1024]{1,0:T(8,128)(2,1)S(1)}, u32[]{:S(2)}, u32[]{:S(2)}) collective-permute-start(bf16[256,1024]{1,0:T(8,128)(2,1)S(1)} %multiply_convert_fusion), channel_id=1, source_target_pairs={{0,1},{1,0},{2,3},{3,2},{4,5},{5,4},{6,7},{7,6},{8,9},{9,8},{10,11... | collective-permute-start | bytes 1572872 | tf_op jit(solution)/shard_map/ppermute | solution.py:55
  138.3 5.9 %collective-permute-start.12 = (bf16[256,1024]{1,0:T(8,128)(2,1)S(1)}, bf16[256,1024]{1,0:T(8,128)(2,1)S(1)}, u32[]{:S(2)}, u32[]{:S(2)}) collective-permute-start(bf16[256,1024]{1,0:T(8,128)(2,1)S(1)} %collective-permute-done.11), channel_id=1, source_target_pairs={{0,1},{1,0},{2,3},{3,2},{4,5},{5,4},{6,7},{7,6},{8,9},{9,8},{10,11... | collective-permute-start | bytes 1572872 | tf_op jit(solution)/shard_map/ppermute | solution.py:55
  145.6 10.5 %collective-permute-start.14 = (bf16[128,2048]{1,0:T(8,128)(2,1)S(1)}, bf16[128,2048]{1,0:T(8,128)(2,1)S(1)}, u32[]{:S(2)}, u32[]{:S(2)}) collective-permute-start(bf16[128,2048]{1,0:T(8,128)(2,1)S(1)} %get-tuple-element.9), channel_id=1, source_target_pairs={{1,4},{3,6},{4,1},{6,3},{9,12},{11,14},{12,9},{14,11},{17,20},{19,... | collective-permute-start | bytes 1572872 | tf_op jit(solution)/shard_map/ppermute | solution.py:79
  147.8 11.7 %collective-permute-start.13 = (bf16[128,2048]{1,0:T(8,128)(2,1)S(1)}, bf16[128,2048]{1,0:T(8,128)(2,1)S(1)}, u32[]{:S(2)}, u32[]{:S(2)}) collective-permute-start(bf16[128,2048]{1,0:T(8,128)(2,1)S(1)} %get-tuple-element.8), channel_id=1, source_target_pairs={{0,1},{1,5},{2,3},{3,7},{4,0},{5,4},{6,2},{7,6},{8,9},{9,13},{10,1... | collective-permute-start | bytes 1572872 | tf_op jit(solution)/shard_map/ppermute | solution.py:79
  149.6 11.0 %collective-permute-start.29 = (bf16[256,1024]{1,0:T(8,128)(2,1)S(1)}, bf16[256,1024]{1,0:T(8,128)(2,1)S(1)}, u32[]{:S(2)}, u32[]{:S(2)}) collective-permute-start(bf16[256,1024]{1,0:T(8,128)(2,1)S(1)} %collective-permute-done.28), channel_id=1, source_target_pairs={{0,1},{1,0},{2,3},{3,2},{4,5},{5,4},{6,7},{7,6},{8,9},{9,8},{10,11... | collective-permute-start | bytes 1572872 | tf_op jit(solution)/shard_map/ppermute | solution.py:55
  159.8 6.7 %collective-permute-start.15 = (bf16[64,2048]{1,0:T(8,128)(2,1)S(1)}, bf16[64,2048]{1,0:T(8,128)(2,1)S(1)}, u32[]{:S(2)}, u32[]{:S(2)}) collective-permute-start(bf16[64,2048]{1,0:T(8,128)(2,1)S(1)} %select_convert_fusion.3), channel_id=1, source_target_pairs={{0,2},{1,3},{2,0},{3,1},{4,6},{5,7},{6,4},{7,5},{8,10},{9,11},{10,... | collective-permute-start | bytes 786440 | tf_op jit(solution)/shard_map/ppermute | solution.py:55
  162.0 16.8 %collective-permute-start.31 = (bf16[128,2048]{1,0:T(8,128)(2,1)S(1)}, bf16[128,2048]{1,0:T(8,128)(2,1)S(1)}, u32[]{:S(2)}, u32[]{:S(2)}) collective-permute-start(bf16[128,2048]{1,0:T(8,128)(2,1)S(1)} %get-tuple-element.11), channel_id=1, source_target_pairs={{1,4},{3,6},{4,1},{6,3},{9,12},{11,14},{12,9},{14,11},{17,20},{19,... | collective-permute-start | bytes 1572872 | tf_op jit(solution)/shard_map/ppermute | solution.py:79
  166.4 14.5 %collective-permute-start.30 = (bf16[128,2048]{1,0:T(8,128)(2,1)S(1)}, bf16[128,2048]{1,0:T(8,128)(2,1)S(1)}, u32[]{:S(2)}, u32[]{:S(2)}) collective-permute-start(bf16[128,2048]{1,0:T(8,128)(2,1)S(1)} %get-tuple-element.10), channel_id=1, source_target_pairs={{0,1},{1,5},{2,3},{3,7},{4,0},{5,4},{6,2},{7,6},{8,9},{9,13},{10,1... | collective-permute-start | bytes 1572872 | tf_op jit(solution)/shard_map/ppermute | solution.py:79
  166.6 17.2 %collective-permute-start.16 = (bf16[64,2048]{1,0:T(8,128)(2,1)S(1)}, bf16[64,2048]{1,0:T(8,128)(2,1)S(1)}, u32[]{:S(2)}, u32[]{:S(2)}) collective-permute-start(bf16[64,2048]{1,0:T(8,128)(2,1)S(1)} %get-tuple-element.4), channel_id=1, source_target_pairs={{0,8},{4,12},{8,0},{12,4},{1,9},{5,13},{9,1},{13,5},{2,10},{6,14},... | collective-permute-start | bytes 786440 | tf_op jit(solution)/shard_map/ppermute | solution.py:59
  186.7 17.3 %collective-permute-start.33 = (bf16[64,2048]{1,0:T(8,128)(2,1)S(1)}, bf16[64,2048]{1,0:T(8,128)(2,1)S(1)}, u32[]{:S(2)}, u32[]{:S(2)}) collective-permute-start(bf16[64,2048]{1,0:T(8,128)(2,1)S(1)} %get-tuple-element.6), channel_id=1, source_target_pairs={{0,8},{4,12},{8,0},{12,4},{1,9},{5,13},{9,1},{13,5},{2,10},{6,14},... | collective-permute-start | bytes 786440 | tf_op jit(solution)/shard_map/ppermute | solution.py:59
  (10 other events, 176.5 us)

commit v3 on v1

v3 whole, which is shorter than its diff:
```python
import functools

import jax
import jax.numpy as jnp
from jax import lax
from jax.experimental import pallas as pl
from jax.experimental.pallas import tpu as pltpu
from jax.sharding import PartitionSpec as P

ROWS = (32, 64, 32)
ORDER = (
    "far0", "sel0", "far1", "arr0", "sel1", "far2", "take0", "a0", "c0", "arr1", "b0", "sel2", "d0", "take1",
    "a1", "c1", "arr2", "hide0", "b1", "d1", "take2", "a2", "own0", "c2", "forward0", "b2", "rest0", "out0",
    "d2", "mix0", "hide1", "far_out0", "own1", "hide2", "end0", "forward1", "own2", "rest1", "out1",
    "forward2", "rest2", "out2", "mix1", "mix2", "far_out1", "far_out2", "end1", "end2",
)
TILE = 256
COST = 1 << 33


def blocks(array):
    return array.reshape(array.shape[0], array.shape[1] // 128, 128)


def block_scale(array):
    return jnp.max(jnp.abs(blocks(array)), axis=2) + 1e-06


def expand(values, scales):
    return (blocks(values.astype(jnp.float32)) * scales[:, :, None]).reshape(values.shape)


def scaled(total):
    scales = block_scale(total)
    values = (blocks(total) / scales[:, :, None]).reshape(total.shape).astype(jnp.bfloat16)
    return values, scales


def wide(array):
    return array.astype(jnp.float32)


def narrow(array):
    return array.astype(jnp.bfloat16)


def dot(a, b):
    return jnp.dot(a, b, preferred_element_type=jnp.float32)


def any_shards(tokens_values, tokens_scales, gate_weight, up_weight, down_weight):
    mine = narrow(expand(tokens_values, tokens_scales))
    mine = lax.all_gather(mine, "tp", axis=1, tiled=True)
    inputs = lax.all_to_all(mine, "seq", split_axis=1, concat_axis=0, tiled=True)
    gate = narrow(dot(inputs, gate_weight))
    up = narrow(dot(inputs, up_weight))
    gate = wide(lax.psum_scatter(gate, "seq", scatter_dimension=0, tiled=True))
    up = wide(lax.psum_scatter(up, "seq", scatter_dimension=0, tiled=True))
    hidden = narrow(jax.nn.silu(gate) * up)
    hidden = lax.all_gather(hidden, "seq", axis=0, tiled=True)
    partial_sum = narrow(dot(hidden, down_weight))
    partial_sum = lax.all_to_all(partial_sum, "seq", split_axis=0, concat_axis=1, tiled=True)
    return scaled(wide(lax.psum_scatter(partial_sum, "tp", scatter_dimension=1, tiled=True)))


def over_seq(array, bit):
    return lax.ppermute(array, "seq", [(i, i ^ bit) for i in range(4)])


def over_tp(array, bit):
    return lax.ppermute(array, "tp", [(i, i ^ bit) for i in range(4)])


def device(tp, seq):
    return tp * 4 + seq


FIRST_IN, SECOND, FIRST_OUT = [], [], []
for tp in range(4):
    for seq in range(4):
        if (tp ^ seq) & 1:
            FIRST_IN.append((device(tp, seq), device(tp, seq ^ 1)))
            SECOND.append((device(tp, seq), device(tp ^ 1, seq ^ 1)))
            FIRST_OUT.append((device(tp, seq), device(tp ^ 1, seq)))
        else:
            FIRST_IN.append((device(tp, seq), device(tp ^ 1, seq)))
            FIRST_OUT.append((device(tp, seq), device(tp, seq ^ 1)))


def over_both(array, pairs):
    return lax.ppermute(array, ("tp", "seq"), pairs)


def arrange(low_first, one, other):
    return jnp.concatenate([jnp.where(low_first, one, other), jnp.where(low_first, other, one)], axis=0)


def sums_kernel(has_got, quarters, some, gate_weight, up_weight, *rest):
    out = rest[-1]
    for k, weight in enumerate((gate_weight, up_weight)):
        value = dot(some[...], weight[...])
        if has_got:
            value += wide(rest[0][0, k])
        out[0, k] = value.astype(out.dtype)


def sums(some, gate_weight, up_weight, quarters, got=None, kind=jnp.bfloat16):
    rows, deep = some.shape
    width = gate_weight.shape[1] // 4
    count, tiles = len(quarters), width // TILE
    pair = pl.BlockSpec((1, 2, rows, TILE), lambda i, j, q: (i, 0, 0, j))
    weight = pl.BlockSpec((deep, TILE), lambda i, j, q: (0, q[i] * tiles + j))
    return pl.pallas_call(
        functools.partial(sums_kernel, got is not None),
        out_shape=jax.ShapeDtypeStruct((count, 2, rows, width), kind),
        grid_spec=pltpu.PrefetchScalarGridSpec(
            num_scalar_prefetch=1,
            grid=(count, tiles),
            in_specs=[pl.BlockSpec((rows, deep), lambda i, j, q: (0, 0)), weight, weight]
            + [pair] * (got is not None),
            out_specs=pair,
        ),
        compiler_params=pltpu.CompilerParams(vmem_limit_bytes=24 << 20),
        cost_estimate=pl.CostEstimate(flops=COST, bytes_accessed=1, transcendentals=0),
    )(jnp.stack(quarters).astype(jnp.int32), some, gate_weight, up_weight, *([] if got is None else [got]))


def products_kernel(quarters, one, two, first_weight, second_weight, *rest):
    value = dot(one[...], first_weight[...]) + dot(two[...], second_weight[...])
    if len(rest) > 1:
        value += rest[0][...]
    rest[-1][...] = value


def products(pieces, weight, quarters, total=None):
    rows, deep = pieces[0].shape
    wide_tile = 2 * TILE
    piece = pl.BlockSpec((rows, deep), lambda j, q: (0, 0))
    out = pl.BlockSpec((rows, wide_tile), lambda j, q: (0, j))
    return pl.pallas_call(
        products_kernel,
        out_shape=jax.ShapeDtypeStruct((rows, weight.shape[1]), jnp.float32),
        grid_spec=pltpu.PrefetchScalarGridSpec(
            num_scalar_prefetch=1,
            grid=(weight.shape[1] // wide_tile,),
            in_specs=[
                piece,
                piece,
                pl.BlockSpec((deep, wide_tile), lambda j, q: (q[0], j)),
                pl.BlockSpec((deep, wide_tile), lambda j, q: (q[1], j)),
            ]
            + [out] * (total is not None),
            out_specs=out,
        ),
        compiler_params=pltpu.CompilerParams(vmem_limit_bytes=24 << 20),
        cost_estimate=pl.CostEstimate(flops=COST, bytes_accessed=1, transcendentals=0),
    )(jnp.stack(quarters).astype(jnp.int32), *pieces, weight, weight, *([] if total is None else [total]))


class Steps:

    def __init__(self, tokens_values, tokens_scales, gate_weight, up_weight, down_weight):
        tp, seq = lax.axis_index("tp"), lax.axis_index("seq")
        self.seq, self.x, self.core = seq, seq >> 1, seq & 1
        self.high, self.even = tp >> 1, (tp ^ seq) & 1 == 0
        self.gate_weight = pltpu.with_memory_space_constraint(gate_weight, pltpu.HBM)
        self.up_weight = pltpu.with_memory_space_constraint(up_weight, pltpu.HBM)
        self.down_weight = pltpu.with_memory_space_constraint(down_weight, pltpu.HBM)
        self.mine = narrow(expand(tokens_values, tokens_scales))
        unit = tokens_values.shape[0] // sum(ROWS)
        self.starts = [sum(ROWS[:i]) * unit for i in range(len(ROWS) + 1)]
        self.last = self.mine
        self.held = {}

    def run(self, order):
        for step in order:
            with jax.named_scope(step):
                getattr(self, step[:-1])(int(step[-1]))
        return tuple(
            jnp.concatenate([self.held["end", i][k] for i in range(len(ROWS))], axis=0) for k in range(2)
        )

    def now(self, array):
        return lax.optimization_barrier((array, self.last))[0]

    def far(self, i):
        part = self.now(self.mine[self.starts[i] : self.starts[i + 1]])
        self.held["far", i] = part, over_tp(part, 2)

    def sel(self, i):
        part, other = self.held["far", i]
        other = self.now(other)
        sent = jnp.where(self.high == self.x, other, part)
        kept = jnp.where(self.high == self.x, part, other)
        self.held["sel", i] = kept, over_seq(sent, 2)
        self.last = sent

    def arr(self, i):
        kept, got = self.held["sel", i]
        pair = arrange(self.x == 0, kept, self.now(got))
        self.held["arr", i] = pair, over_both(pair, FIRST_IN), over_both(pair, SECOND)
        self.last = pair

    def take(self, i):
        pair, first, second = self.held["arr", i]
        first = self.now(first)
        own = jnp.where(self.even, pair, first)
        others = jnp.where(self.even, first, second)
        self.held["take", i] = self.last = arrange(self.core == 0, own, others)

    def part(self, i, bits, got=None, kind=jnp.bfloat16):
        some = self.now(self.held["take", i])
        quarters = [self.seq ^ bit for bit in bits]
        self.last = sums(some, self.gate_weight, self.up_weight, quarters, got, kind)
        return self.last

    def a(self, i):
        self.held["a", i] = over_seq(self.part(i, (3,)), 1)

    def c(self, i):
        self.held["c", i] = over_seq(self.part(i, (1,)), 1)

    def b(self, i):
        self.held["b", i] = over_seq(self.part(i, (2,), self.held["a", i]), 2)

    def d(self, i):
        self.held["d", i] = self.part(i, (0,), self.held["c", i], jnp.float32)

    def hide(self, i):
        gate, up = (self.held["d", i] + wide(self.now(self.held["b", i])))[0]
        hidden = narrow(jax.nn.silu(gate) * up)
        far = over_seq(hidden, 2)
        self.held["hide", i] = hidden, far, over_seq(hidden, 1)
        self.last = hidden

    def down(self, pieces, bits, total=None):
        return products(pieces, self.down_weight, [self.seq ^ bit for bit in bits], total)

    def own(self, i):
        hidden, far, near = self.held["hide", i]
        self.held["own", i] = self.last = self.down((self.now(hidden), near), (0, 1))

    def forward(self, i):
        far = self.now(self.held["hide", i][1])
        self.held["pass", i] = far, over_seq(far, 1)

    def rest(self, i):
        far, last = self.held["pass", i]
        self.held["rest", i] = self.last = self.down((self.now(far), last), (2, 3), self.held["own", i])

    def out(self, i):
        partial_sum = self.now(self.held["rest", i])
        half = partial_sum.shape[0] // 2
        low, top = partial_sum[:half], partial_sum[half:]
        own = jnp.where(self.core == 0, low, top)
        others = jnp.where(self.core == 0, top, low)
        one, two = narrow(jnp.where(self.even, others, own)), narrow(others)
        self.held["out", i] = own, over_both(one, FIRST_OUT), over_both(two, SECOND)
        self.last = one

    def mix(self, i):
        own, first, second = self.held["out", i]
        pair = wide(self.now(first)) + jnp.where(self.even, own, wide(second))
        rows = pair.shape[0] // 2
        low, top = pair[:rows], pair[rows:]
        kept = jnp.where(self.x == 0, low, top)
        sent = narrow(jnp.where(self.x == 0, top, low))
        self.held["mix", i] = kept, over_seq(sent, 2)
        self.last = sent

    def far_out(self, i):
        kept, got = self.held["mix", i]
        got = self.now(got)
        sent = jnp.where(self.high == self.x, got, narrow(kept))
        kept = jnp.where(self.high == self.x, kept, wide(got))
        self.held["far_out", i] = kept, over_tp(sent, 2)
        self.last = sent

    def end(self, i):
        kept, got = self.held["far_out", i]
        self.held["end", i] = scaled(kept + wide(self.now(got)))
        self.last = self.held["end", i][0]


def four_shards(*arrays):
    return Steps(*arrays).run(ORDER)


def solution(mesh):
    placed = (
        P(("groups", "seq"), "tp"),
        P(("groups", "seq"), "tp"),
        P("seq", "tp"),
        P("seq", "tp"),
        P("tp", "seq"),
    )
    fours = mesh.shape["tp"] == 4 and mesh.shape["seq"] == 4
    return jax.shard_map(
        four_shards if fours else any_shards,
        mesh=mesh,
        in_specs=placed,
        out_specs=(P(("groups", "seq"), "tp"), P(("groups", "seq"), "tp")),
        check_vma=False,
    )
```

time: 331 us -> 218 us (0.66)
  waiting for transfers between devices: 201 us -> 61.7 us
  Pallas kernels: 0 us -> 96.1 us
  blocking collectives: 56.3 us -> 0 us
  starting transfers between devices: 0.21 us -> 44.9 us
  matrix products: 42.3 us -> 0 us
  between operations: 13.8 us -> 1.46 us
  local copies, waits for them, and re-layouts: 8.21 us -> 3.76 us
    reduce_scatter x3 -> x0, waiting for transfers between devices: 118 us -> none  [the longest x1 47.2 us: shards(): lax.psum_scatter(gate, 'seq', scatter_dimension=0, tiled=True)]
    pallas_call x0 -> x18, Pallas kernels: none -> 96.1 us  [the longest x12 61.8 us: sums(): pl.pallas_call(functools.partial(sums_kernel, got is not None), out_shape...]
    all_gather x2 -> x0, waiting for transfers between devices: 83.1 us -> none  [the longest x1 48.1 us: shards(): mine = lax.all_gather(mine, 'tp', axis=1, tiled=True)]
    ppermute x0 -> x42, waiting for transfers between devices: none -> 61.7 us  [the longest x6 26.9 us: over_tp(): return lax.ppermute(array, 'tp', [(i, i ^ bit) for i in range(4)])]
    all_to_all x2 -> x0, blocking collectives: 56.3 us -> none  [the longest x1 28.9 us: shards(): lax.all_to_all(mine, 'seq', split_axis=1, concat_axis=0, tiled=True)]
    ppermute x0 -> x42, starting transfers between devices: none -> 44.9 us  [the longest x12 19 us: over_both(): return lax.ppermute(array, ('tp', 'seq'), pairs)]
    dot_general x3 -> x0, matrix products: 42.3 us -> none  [the longest x1 14.4 us: shards(): jnp.dot(inputs, gate_weight, preferred_element_type=jnp.float32)]
    all_to_all x2 -> x0, local copies, waits for them, and re-layouts: 4.2 us -> none  [the longest x1 2.72 us: shards(): lax.all_to_all(mine, 'seq', split_axis=1, concat_axis=0, tiled=True)]
  transfers between devices with their start and end apart: 5 -> 42, of which waited for: 5 -> 16; matrix products, arithmetic and copies ran while one was open for 4% -> 3% of each run, Pallas kernels for 0% -> 44%
where the time goes in v3:
time: 218 us; the launch traced here: 216 us
  Pallas kernels  96.1 us (44%)
  waiting for transfers between devices  61.7 us (28%)
  starting transfers between devices  44.9 us (21%)
  other arithmetic  8.4 us (4%)
  local copies, waits for them, and re-layouts  3.76 us (2%)
    pallas_call x12, Pallas kernels, sums(): pl.pallas_call(functools.partial(sums_kernel, got is not None), out_shape...  61.8 us
    pallas_call x6, Pallas kernels, products(): pl.pallas_call(products_kernel, out_shape=jax.ShapeDtypeStruct((rows, wei...  34.3 us
    ppermute x6, waiting for transfers between devices, over_tp(): return lax.ppermute(array, 'tp', [(i, i ^ bit) for i in range(4)])  26.9 us
    ppermute x24, waiting for transfers between devices, over_seq(): return lax.ppermute(array, 'seq', [(i, i ^ bit) for i in range(4)])  21.6 us
    ppermute x12, starting transfers between devices, over_both(): return lax.ppermute(array, ('tp', 'seq'), pairs)  19 us
    ppermute x24, starting transfers between devices, over_seq(): return lax.ppermute(array, 'seq', [(i, i ^ bit) for i in range(4)])  17.8 us
    ppermute x12, waiting for transfers between devices, over_both(): return lax.ppermute(array, ('tp', 'seq'), pairs)  13.3 us
    ppermute x6, starting transfers between devices, over_tp(): return lax.ppermute(array, 'tp', [(i, i ^ bit) for i in range(4)])  8.12 us
  transfers between devices with their start and end apart: 42, of which 16 were waited for; matrix products, arithmetic and copies ran while one was open for 3% of the time, Pallas kernels for 44%

profile of v3, /device:TPU:1, one launch (start us, length us, event | category | flops | bytes accessed | tf_op | source)
XLA Modules:
  0.0 216.3 jit_solution(9784797012927652219)
XLA Ops:
  3.2 3.2 %collective-permute-start = (bf16[32,2048]{1,0:T(8,128)(2,1)S(1)}, bf16[32,2048]{1,0:T(8,128)(2,1)S(1)}, u32[]{:S(2)}, u32[]{:S(2)}) collective-permute-start(bf16[32,2048]{1,0:T(8,128)(2,1)S(1)} %get-tuple-element.47), channel_id=1, source_target_pairs={{0,8},{4,12},{8,0},{12,4},{1,9},{5,13},{9,1},{13,5},{2,10},{6,14},... | collective-permute-start | bytes 393224 | tf_op jit(solution)/shard_map/far0/ppermute | solution.py:71
  6.4 6.0 %collective-permute-done = bf16[32,2048]{1,0:T(8,128)(2,1)S(1)} collective-permute-done((bf16[32,2048]{1,0:T(8,128)(2,1)S(1)}, bf16[32,2048]{1,0:T(8,128)(2,1)S(1)}, u32[]{:S(2)}, u32[]{:S(2)}) %collective-permute-start) | collective-permute-done | bytes 131104 | tf_op jit(solution)/shard_map/far0/ppermute | solution.py:71
  13.7 2.6 %collective-permute-done.1 = bf16[32,2048]{1,0:T(8,128)(2,1)S(1)} collective-permute-done((bf16[32,2048]{1,0:T(8,128)(2,1)S(1)}, bf16[32,2048]{1,0:T(8,128)(2,1)S(1)}, u32[]{:S(2)}, u32[]{:S(2)}) %collective-permute-start.1) | collective-permute-done | bytes 131104 | tf_op jit(solution)/shard_map/sel0/ppermute | solution.py:67
  16.4 5.1 %collective-permute-start.4 = (bf16[64,2048]{1,0:T(8,128)(2,1)S(1)}, bf16[64,2048]{1,0:T(8,128)(2,1)S(1)}, u32[]{:S(2)}, u32[]{:S(2)}) collective-permute-start(bf16[64,2048]{1,0:T(8,128)(2,1)S(1)} %pad_maximum_fusion.5), channel_id=1, source_target_pairs={{1,4},{3,6},{4,1},{6,3},{9,12},{11,14},{12,9},{14,11},{17,20},{19,... | collective-permute-start | bytes 786440 | tf_op jit(solution)/shard_map/arr0/ppermute | solution.py:91
  21.5 5.0 %collective-permute-done.3 = bf16[64,2048]{1,0:T(8,128)(2,1)S(1)} collective-permute-done((bf16[64,2048]{1,0:T(8,128)(2,1)S(1)}, bf16[64,2048]{1,0:T(8,128)(2,1)S(1)}, u32[]{:S(2)}, u32[]{:S(2)}) %collective-permute-start.3) | collective-permute-done | bytes 262176 | tf_op jit(solution)/shard_map/far1/ppermute | solution.py:71
  27.4 5.4 %collective-permute-done.2 = bf16[64,2048]{1,0:T(8,128)(2,1)S(1)} collective-permute-done((bf16[64,2048]{1,0:T(8,128)(2,1)S(1)}, bf16[64,2048]{1,0:T(8,128)(2,1)S(1)}, u32[]{:S(2)}, u32[]{:S(2)}) %collective-permute-start.2) | collective-permute-done | bytes 262176 | tf_op jit(solution)/shard_map/arr0/ppermute | solution.py:91
  33.0 4.9 %a0.1 = bf16[1,2,128,1024]{3,2,1,0:T(8,128)(2,1)S(1)} custom-call(s32[1]{0:T(128)} %bitcast.1.quarters, bf16[128,2048]{1,0:T(8,128)(2,1)S(1)} %pad_maximum_fusion.1.some, bf16[2048,4096]{1,0:T(8,128)(2,1)} %gate_weight.23, bf16[2048,4096]{1,0:T(8,128)(2,1)} %up_weight.23), custom_call_target="tpu_custom_call" | custom-call | flops 8589934592 | bytes 1 | tf_op jit(solution)/shard_map/a0/pallas_call | solution.py:113
  38.0 4.9 %c0.1 = bf16[1,2,128,1024]{3,2,1,0:T(8,128)(2,1)S(1)} custom-call(s32[1]{0:T(128)} %bitcast.3.quarters, bf16[128,2048]{1,0:T(8,128)(2,1)S(1)} %pad_maximum_fusion.1.some, bf16[2048,4096]{1,0:T(8,128)(2,1)} %gate_weight.23, bf16[2048,4096]{1,0:T(8,128)(2,1)} %up_weight.23), custom_call_target="tpu_custom_call" | custom-call | flops 8589934592 | bytes 1 | tf_op jit(solution)/shard_map/c0/pallas_call | solution.py:113
  45.6 4.9 %b0.1 = bf16[1,2,128,1024]{3,2,1,0:T(8,128)(2,1)S(1)} custom-call(s32[1]{0:T(128)} %bitcast.quarters, bf16[128,2048]{1,0:T(8,128)(2,1)S(1)} %pad_maximum_fusion.1.some, bf16[2048,4096]{1,0:T(8,128)(2,1)} %gate_weight.23, bf16[2048,4096]{1,0:T(8,128)(2,1)} %up_weight.23, bf16[1,2,128,1024]{3,2,1,0:T(8,128)(2,1)S(1)} %collective-permute-done.7.rest_0_), custom_call_target="tpu_custom_call" | custom-call | flops 8589934592 | bytes 1 | tf_op jit(solution)/shard_map/b0/pallas_call | solution.py:113
  52.7 4.9 %d0.1 = f32[1,2,128,1024]{3,2,1,0:T(8,128)S(1)} custom-call(s32[1]{0:T(128)} %bitcast.2.quarters, bf16[128,2048]{1,0:T(8,128)(2,1)S(1)} %pad_maximum_fusion.1.some, bf16[2048,4096]{1,0:T(8,128)(2,1)} %gate_weight.23, bf16[2048,4096]{1,0:T(8,128)(2,1)} %up_weight.23, bf16[1,2,128,1024]{3,2,1,0:T(8,128)(2,1)S(1)} %collective-permute-done.8.rest_0_), custom_call_target="tpu_custom_call" | custom-call | flops 8589934592 | bytes 1 | tf_op jit(solution)/shard_map/d0/pallas_call | solution.py:113
  59.9 5.6 %a1.1 = bf16[1,2,256,1024]{3,2,1,0:T(8,128)(2,1)S(1)} custom-call(s32[1]{0:T(128)} %bitcast.1.quarters, bf16[256,2048]{1,0:T(8,128)(2,1)S(1)} %pad_maximum_fusion.some, bf16[2048,4096]{1,0:T(8,128)(2,1)} %gate_weight.23, bf16[2048,4096]{1,0:T(8,128)(2,1)} %up_weight.23), custom_call_target="tpu_custom_call" | custom-call | flops 8589934592 | bytes 1 | tf_op jit(solution)/shard_map/a1/pallas_call | solution.py:113
  66.0 5.5 %c1.1 = bf16[1,2,256,1024]{3,2,1,0:T(8,128)(2,1)S(1)} custom-call(s32[1]{0:T(128)} %bitcast.3.quarters, bf16[256,2048]{1,0:T(8,128)(2,1)S(1)} %pad_maximum_fusion.some, bf16[2048,4096]{1,0:T(8,128)(2,1)} %gate_weight.23, bf16[2048,4096]{1,0:T(8,128)(2,1)} %up_weight.23), custom_call_target="tpu_custom_call" | custom-call | flops 8589934592 | bytes 1 | tf_op jit(solution)/shard_map/c1/pallas_call | solution.py:113
  77.9 5.6 %b1.1 = bf16[1,2,256,1024]{3,2,1,0:T(8,128)(2,1)S(1)} custom-call(s32[1]{0:T(128)} %bitcast.quarters, bf16[256,2048]{1,0:T(8,128)(2,1)S(1)} %pad_maximum_fusion.some, bf16[2048,4096]{1,0:T(8,128)(2,1)} %gate_weight.23, bf16[2048,4096]{1,0:T(8,128)(2,1)} %up_weight.23, bf16[1,2,256,1024]{3,2,1,0:T(8,128)(2,1)S(1)} %collective-permute-done.15.rest_0_), custom_call_target="tpu_custom_call" | custom-call | flops 8589934592 | bytes 1 | tf_op jit(solution)/shard_map/b1/pallas_call | solution.py:113
  83.5 5.7 %d1.1 = f32[1,2,256,1024]{3,2,1,0:T(8,128)S(1)} custom-call(s32[1]{0:T(128)} %bitcast.2.quarters, bf16[256,2048]{1,0:T(8,128)(2,1)S(1)} %pad_maximum_fusion.some, bf16[2048,4096]{1,0:T(8,128)(2,1)} %gate_weight.23, bf16[2048,4096]{1,0:T(8,128)(2,1)} %up_weight.23, bf16[1,2,256,1024]{3,2,1,0:T(8,128)(2,1)S(1)} %collective-permute-done.16.rest_0_), custom_call_target="tpu_custom_call" | custom-call | flops 8589934592 | bytes 1 | tf_op jit(solution)/shard_map/d1/pallas_call | solution.py:113
  89.4 4.9 %a2.1 = bf16[1,2,128,1024]{3,2,1,0:T(8,128)(2,1)S(1)} custom-call(s32[1]{0:T(128)} %bitcast.1.quarters, bf16[128,2048]{1,0:T(8,128)(2,1)S(1)} %pad_maximum_fusion.3.some, bf16[2048,4096]{1,0:T(8,128)(2,1)} %gate_weight.23, bf16[2048,4096]{1,0:T(8,128)(2,1)} %up_weight.23), custom_call_target="tpu_custom_call" | custom-call | flops 8589934592 | bytes 1 | tf_op jit(solution)/shard_map/a2/pallas_call | solution.py:113
  95.1 5.5 %own0.1.rest_0_ = f32[128,2048]{1,0:T(8,128)S(1)} custom-call(s32[2]{0:T(128)S(1)} %pad_add_fusion.1.quarters, bf16[128,1024]{1,0:T(8,128)(2,1)S(1)} %fusion.7.one, bf16[128,1024]{1,0:T(8,128)(2,1)S(1)} %collective-permute-done.18.two, bf16[4096,2048]{1,0:T(8,128)(2,1)} %second_weight.11, bf16[4096,2048]{1,0:T(8,128)(2,1)} %second_weight.11), custom_call_target="tpu_custom_call" | custom-call | flops 8589934592 | bytes 1 | tf_op jit(solution)/shard_map/own0/pallas_call | solution.py:140
  100.6 4.9 %c2.1 = bf16[1,2,128,1024]{3,2,1,0:T(8,128)(2,1)S(1)} custom-call(s32[1]{0:T(128)} %bitcast.3.quarters, bf16[128,2048]{1,0:T(8,128)(2,1)S(1)} %pad_maximum_fusion.3.some, bf16[2048,4096]{1,0:T(8,128)(2,1)} %gate_weight.23, bf16[2048,4096]{1,0:T(8,128)(2,1)} %up_weight.23), custom_call_target="tpu_custom_call" | custom-call | flops 8589934592 | bytes 1 | tf_op jit(solution)/shard_map/c2/pallas_call | solution.py:113
  106.2 4.9 %b2.1 = bf16[1,2,128,1024]{3,2,1,0:T(8,128)(2,1)S(1)} custom-call(s32[1]{0:T(128)} %bitcast.quarters, bf16[128,2048]{1,0:T(8,128)(2,1)S(1)} %pad_maximum_fusion.3.some, bf16[2048,4096]{1,0:T(8,128)(2,1)} %gate_weight.23, bf16[2048,4096]{1,0:T(8,128)(2,1)} %up_weight.23, bf16[1,2,128,1024]{3,2,1,0:T(8,128)(2,1)S(1)} %collective-permute-done.19.rest_0_), custom_call_target="tpu_custom_call" | custom-call | flops 8589934592 | bytes 1 | tf_op jit(solution)/shard_map/b2/pallas_call | solution.py:113
  111.1 5.5 %rest0.1 = f32[128,2048]{1,0:T(8,128)S(1)} custom-call(s32[2]{0:T(128)S(1)} %pad_add_fusion.quarters, bf16[128,1024]{1,0:T(8,128)(2,1)S(1)} %collective-permute-done.13.one, bf16[128,1024]{1,0:T(8,128)(2,1)S(1)} %collective-permute-done.20.two, bf16[4096,2048]{1,0:T(8,128)(2,1)} %second_weight.11, bf16[4096,2048]{1,0:T(8,128)(2,1)} %second_weight.11, ...), custom_call_target="tpu_custom_call" | custom-call | flops 8589934592 | bytes 1 | tf_op jit(solution)/shard_map/rest0/pallas_call | solution.py:140
  116.8 3.8 %collective-permute-start.23 = (bf16[64,2048]{1,0:T(8,128)(2,1)S(1)}, bf16[64,2048]{1,0:T(8,128)(2,1)S(1)}, u32[]{:S(2)}, u32[]{:S(2)}) collective-permute-start(bf16[64,2048]{1,0:T(8,128)(2,1)S(1)} %get-tuple-element.106), channel_id=1, source_target_pairs={{1,4},{3,6},{4,1},{6,3},{9,12},{11,14},{12,9},{14,11},{17,20},{19,... | collective-permute-start | bytes 786440 | tf_op jit(solution)/shard_map/out0/ppermute | solution.py:91
  120.6 4.9 %d2.1 = f32[1,2,128,1024]{3,2,1,0:T(8,128)S(1)} custom-call(s32[1]{0:T(128)} %bitcast.2.quarters, bf16[128,2048]{1,0:T(8,128)(2,1)S(1)} %pad_maximum_fusion.3.some, bf16[2048,4096]{1,0:T(8,128)(2,1)} %gate_weight.23, bf16[2048,4096]{1,0:T(8,128)(2,1)} %up_weight.23, bf16[1,2,128,1024]{3,2,1,0:T(8,128)(2,1)S(1)} %collective-permute-done.22.rest_0_), custom_call_target="tpu_custom_call" | custom-call | flops 8589934592 | bytes 1 | tf_op jit(solution)/shard_map/d2/pallas_call | solution.py:113
  135.4 6.1 %own1.1.rest_0_ = f32[256,2048]{1,0:T(8,128)S(1)} custom-call(s32[2]{0:T(128)S(1)} %pad_add_fusion.1.quarters, bf16[256,1024]{1,0:T(8,128)(2,1)S(1)} %fusion.2.one, bf16[256,1024]{1,0:T(8,128)(2,1)S(1)} %collective-permute-done.28.two, bf16[4096,2048]{1,0:T(8,128)(2,1)} %second_weight.11, bf16[4096,2048]{1,0:T(8,128)(2,1)} %second_weight.11), custom_call_target="tpu_custom_call" | custom-call | flops 8589934592 | bytes 1 | tf_op jit(solution)/shard_map/own1/pallas_call | solution.py:140
  141.6 4.7 %collective-permute-done.27 = bf16[1,2,128,1024]{3,2,1,0:T(8,128)(2,1)S(1)} collective-permute-done((bf16[1,2,128,1024]{3,2,1,0:T(8,128)(2,1)S(1)}, bf16[1,2,128,1024]{3,2,1,0:T(8,128)(2,1)S(1)}, u32[]{:S(2)}, u32[]{:S(2)}) %collective-permute-start.27) | collective-permute-done | bytes 524320 | tf_op jit(solution)/shard_map/b2/ppermute | solution.py:67
  148.7 8.8 %collective-permute-done.29.one = bf16[256,1024]{1,0:T(8,128)(2,1)S(1)} collective-permute-done((bf16[256,1024]{1,0:T(8,128)(2,1)S(1)}, bf16[256,1024]{1,0:T(8,128)(2,1)S(1)}, u32[]{:S(2)}, u32[]{:S(2)}) %collective-permute-start.29) | collective-permute-done | bytes 524320 | tf_op jit(solution)/shard_map/hide1/ppermute | solution.py:67
  158.8 5.4 %own2.1.rest_0_ = f32[128,2048]{1,0:T(8,128)S(1)} custom-call(s32[2]{0:T(128)S(1)} %pad_add_fusion.1.quarters, bf16[128,1024]{1,0:T(8,128)(2,1)S(1)} %fusion.5.one, bf16[128,1024]{1,0:T(8,128)(2,1)S(1)} %collective-permute-done.30.two, bf16[4096,2048]{1,0:T(8,128)(2,1)} %second_weight.11, bf16[4096,2048]{1,0:T(8,128)(2,1)} %second_weight.11), custom_call_target="tpu_custom_call" | custom-call | flops 8589934592 | bytes 1 | tf_op jit(solution)/shard_map/own2/pallas_call | solution.py:140
  165.4 6.2 %rest1.1 = f32[256,2048]{1,0:T(8,128)S(1)} custom-call(s32[2]{0:T(128)S(1)} %pad_add_fusion.quarters, bf16[256,1024]{1,0:T(8,128)(2,1)S(1)} %copy-done.3, bf16[256,1024]{1,0:T(8,128)(2,1)S(1)} %collective-permute-done.31.two, bf16[4096,2048]{1,0:T(8,128)(2,1)} %second_weight.11, bf16[4096,2048]{1,0:T(8,128)(2,1)} %second_weight.11, f32[256,2048]{1,0:T(8,128)S(1)} %copy-done.1), custom_call_target="tpu_custom_call" | custom-call | flops 8589934592 | bytes 1 | tf_op jit(solution)/shard_map/rest1/pallas_call | solution.py:140
  173.4 4.0 %collective-permute-start.35 = (bf16[128,2048]{1,0:T(8,128)(2,1)}, bf16[128,2048]{1,0:T(8,128)(2,1)S(1)}, u32[]{:S(2)}, u32[]{:S(2)}) collective-permute-start(bf16[128,2048]{1,0:T(8,128)(2,1)} %get-tuple-element.100), channel_id=1, source_target_pairs={{1,4},{3,6},{4,1},{6,3},{9,12},{11,14},{12,9},{14,11},{17,20},{19,... | collective-permute-start | bytes 1572872 | tf_op jit(solution)/shard_map/out1/ppermute | solution.py:91
  177.5 5.5 %rest2.1 = f32[128,2048]{1,0:T(8,128)S(1)} custom-call(s32[2]{0:T(128)S(1)} %pad_add_fusion.quarters, bf16[128,1024]{1,0:T(8,128)(2,1)} %collective-permute-done.33.one, bf16[128,1024]{1,0:T(8,128)(2,1)S(1)} %collective-permute-done.34.two, bf16[4096,2048]{1,0:T(8,128)(2,1)} %second_weight.11, bf16[4096,2048]{1,0:T(8,128)(2,1)} %second_weight.11, ...), custom_call_target="tpu_custom_call" | custom-call | flops 8589934592 | bytes 1 | tf_op jit(solution)/shard_map/rest2/pallas_call | solution.py:140
  185.1 3.1 %collective-permute-done.35 = bf16[128,2048]{1,0:T(8,128)(2,1)S(1)} collective-permute-done((bf16[128,2048]{1,0:T(8,128)(2,1)}, bf16[128,2048]{1,0:T(8,128)(2,1)S(1)}, u32[]{:S(2)}, u32[]{:S(2)}) %collective-permute-start.35) | collective-permute-done | bytes 524320 | tf_op jit(solution)/shard_map/out1/ppermute | solution.py:91
  188.6 2.5 %collective-permute-done.37 = bf16[64,2048]{1,0:T(8,128)(2,1)S(1)} collective-permute-done((bf16[64,2048]{1,0:T(8,128)(2,1)S(1)}, bf16[64,2048]{1,0:T(8,128)(2,1)S(1)}, u32[]{:S(2)}, u32[]{:S(2)}) %collective-permute-start.37) | collective-permute-done | bytes 262176 | tf_op jit(solution)/shard_map/out2/ppermute | solution.py:91
  191.6 2.9 %collective-permute-done.36 = bf16[64,2048]{1,0:T(8,128)(2,1)S(1)} collective-permute-done((bf16[64,2048]{1,0:T(8,128)(2,1)S(1)}, bf16[64,2048]{1,0:T(8,128)(2,1)S(1)}, u32[]{:S(2)}, u32[]{:S(2)}) %collective-permute-start.36) | collective-permute-done | bytes 262176 | tf_op jit(solution)/shard_map/mix1/ppermute | solution.py:67
  197.4 14.0 %collective-permute-done.39 = bf16[64,2048]{1,0:T(8,128)(2,1)S(1)} collective-permute-done((bf16[64,2048]{1,0:T(8,128)(2,1)S(1)}, bf16[64,2048]{1,0:T(8,128)(2,1)S(1)}, u32[]{:S(2)}, u32[]{:S(2)}) %collective-permute-start.39) | collective-permute-done | bytes 262176 | tf_op jit(solution)/shard_map/far_out1/ppermute | solution.py:71
  (143 shorter events, 47.6 us)
Async XLA Ops:
  3.2 9.2 %collective-permute-start = (bf16[32,2048]{1,0:T(8,128)(2,1)S(1)}, bf16[32,2048]{1,0:T(8,128)(2,1)S(1)}, u32[]{:S(2)}, u32[]{:S(2)}) collective-permute-start(bf16[32,2048]{1,0:T(8,128)(2,1)S(1)} %get-tuple-element.47), channel_id=1, source_target_pairs={{0,8},{4,12},{8,0},{12,4},{1,9},{5,13},{9,1},{13,5},{2,10},{6,14},... | collective-permute-start | bytes 393224 | tf_op jit(solution)/shard_map/far0/ppermute | solution.py:71
  13.7 12.8 %collective-permute-start.3 = (bf16[64,2048]{1,0:T(8,128)(2,1)S(1)}, bf16[64,2048]{1,0:T(8,128)(2,1)S(1)}, u32[]{:S(2)}, u32[]{:S(2)}) collective-permute-start(bf16[64,2048]{1,0:T(8,128)(2,1)S(1)} %slice.67), channel_id=1, source_target_pairs={{0,8},{4,12},{8,0},{12,4},{1,9},{5,13},{9,1},{13,5},{2,10},{6,14},... | collective-permute-start | bytes 786440 | tf_op jit(solution)/shard_map/far1/ppermute | solution.py:71
  16.4 16.4 %collective-permute-start.4 = (bf16[64,2048]{1,0:T(8,128)(2,1)S(1)}, bf16[64,2048]{1,0:T(8,128)(2,1)S(1)}, u32[]{:S(2)}, u32[]{:S(2)}) collective-permute-start(bf16[64,2048]{1,0:T(8,128)(2,1)S(1)} %pad_maximum_fusion.5), channel_id=1, source_target_pairs={{1,4},{3,6},{4,1},{6,3},{9,12},{11,14},{12,9},{14,11},{17,20},{19,... | collective-permute-start | bytes 786440 | tf_op jit(solution)/shard_map/arr0/ppermute | solution.py:91
  21.4 11.3 %collective-permute-start.2 = (bf16[64,2048]{1,0:T(8,128)(2,1)S(1)}, bf16[64,2048]{1,0:T(8,128)(2,1)S(1)}, u32[]{:S(2)}, u32[]{:S(2)}) collective-permute-start(bf16[64,2048]{1,0:T(8,128)(2,1)S(1)} %pad_maximum_fusion.5), channel_id=1, source_target_pairs={{0,4},{1,0},{2,6},{3,2},{4,5},{5,1},{6,7},{7,3},{8,12},{9,8},{10,1... | collective-permute-start | bytes 786440 | tf_op jit(solution)/shard_map/arr0/ppermute | solution.py:91
  26.5 16.9 %collective-permute-start.6 = (bf16[64,2048]{1,0:T(8,128)(2,1)S(1)}, bf16[64,2048]{1,0:T(8,128)(2,1)S(1)}, u32[]{:S(2)}, u32[]{:S(2)}) collective-permute-start(bf16[64,2048]{1,0:T(8,128)(2,1)S(1)} %broadcast_select_fusion.7), channel_id=1, source_target_pairs={{0,2},{1,3},{2,0},{3,1},{4,6},{5,7},{6,4},{7,5},{8,10},{9,11},{10,... | collective-permute-start | bytes 786440 | tf_op jit(solution)/shard_map/sel1/ppermute | solution.py:67
  27.4 23.2 %collective-permute-start.5 = (bf16[32,2048]{1,0:T(8,128)(2,1)S(1)}, bf16[32,2048]{1,0:T(8,128)(2,1)S(1)}, u32[]{:S(2)}, u32[]{:S(2)}) collective-permute-start(bf16[32,2048]{1,0:T(8,128)(2,1)S(1)} %get-tuple-element.53), channel_id=1, source_target_pairs={{0,8},{4,12},{8,0},{12,4},{1,9},{5,13},{9,1},{13,5},{2,10},{6,14},... | collective-permute-start | bytes 393224 | tf_op jit(solution)/shard_map/far2/ppermute | solution.py:71
  42.9 9.8 %collective-permute-start.8 = (bf16[1,2,128,1024]{3,2,1,0:T(8,128)(2,1)S(1)}, bf16[1,2,128,1024]{3,2,1,0:T(8,128)(2,1)S(1)}, u32[]{:S(2)}, u32[]{:S(2)}) collective-permute-start(bf16[1,2,128,1024]{3,2,1,0:T(8,128)(2,1)S(1)} %c0.1), channel_id=1, source_target_pairs={{0,1},{1,0},{2,3},{3,2},{4,5},{5,4},{6,7},{7,6},{8,9},{9,8},{10,11... | collective-permute-start | bytes 1572872 | tf_op jit(solution)/shard_map/c0/ppermute | solution.py:67
  43.6 15.9 %collective-permute-start.12 = (bf16[128,2048]{1,0:T(8,128)(2,1)S(1)}, bf16[128,2048]{1,0:T(8,128)(2,1)S(1)}, u32[]{:S(2)}, u32[]{:S(2)}) collective-permute-start(bf16[128,2048]{1,0:T(8,128)(2,1)S(1)} %pad_maximum_fusion.2), channel_id=1, source_target_pairs={{1,4},{3,6},{4,1},{6,3},{9,12},{11,14},{12,9},{14,11},{17,20},{19,... | collective-permute-start | bytes 1572872 | tf_op jit(solution)/shard_map/arr1/ppermute | solution.py:91
  45.5 13.6 %collective-permute-start.11 = (bf16[128,2048]{1,0:T(8,128)(2,1)S(1)}, bf16[128,2048]{1,0:T(8,128)(2,1)S(1)}, u32[]{:S(2)}, u32[]{:S(2)}) collective-permute-start(bf16[128,2048]{1,0:T(8,128)(2,1)S(1)} %pad_maximum_fusion.2), channel_id=1, source_target_pairs={{0,4},{1,0},{2,6},{3,2},{4,5},{5,1},{6,7},{7,3},{8,12},{9,8},{10,1... | collective-permute-start | bytes 1572872 | tf_op jit(solution)/shard_map/arr1/ppermute | solution.py:91
  50.6 21.0 %collective-permute-start.10 = (bf16[32,2048]{1,0:T(8,128)(2,1)S(1)}, bf16[32,2048]{1,0:T(8,128)(2,1)S(1)}, u32[]{:S(2)}, u32[]{:S(2)}) collective-permute-start(bf16[32,2048]{1,0:T(8,128)(2,1)S(1)} %broadcast_select_fusion.21), channel_id=1, source_target_pairs={{0,2},{1,3},{2,0},{3,1},{4,6},{5,7},{6,4},{7,5},{8,10},{9,11},{10,... | collective-permute-start | bytes 393224 | tf_op jit(solution)/shard_map/sel2/ppermute | solution.py:67
  52.6 23.1 %collective-permute-start.9 = (bf16[1,2,128,1024]{3,2,1,0:T(8,128)(2,1)S(1)}, bf16[1,2,128,1024]{3,2,1,0:T(8,128)(2,1)S(1)}, u32[]{:S(2)}, u32[]{:S(2)}) collective-permute-start(bf16[1,2,128,1024]{3,2,1,0:T(8,128)(2,1)S(1)} %b0.1), channel_id=1, source_target_pairs={{0,2},{1,3},{2,0},{3,1},{4,6},{5,7},{6,4},{7,5},{8,10},{9,11},{10,... | collective-permute-start | bytes 1572872 | tf_op jit(solution)/shard_map/b0/ppermute | solution.py:67
  65.5 10.7 %collective-permute-start.15 = (bf16[1,2,256,1024]{3,2,1,0:T(8,128)(2,1)S(1)}, bf16[1,2,256,1024]{3,2,1,0:T(8,128)(2,1)S(1)}, u32[]{:S(2)}, u32[]{:S(2)}) collective-permute-start(bf16[1,2,256,1024]{3,2,1,0:T(8,128)(2,1)S(1)} %a1.1), channel_id=1, source_target_pairs={{0,1},{1,0},{2,3},{3,2},{4,5},{5,4},{6,7},{7,6},{8,9},{9,8},{10,11... | collective-permute-start | bytes 3145736 | tf_op jit(solution)/shard_map/a1/ppermute | solution.py:67
  71.6 17.5 %collective-permute-start.17 = (bf16[64,2048]{1,0:T(8,128)(2,1)S(1)}, bf16[64,2048]{1,0:T(8,128)(2,1)S(1)}, u32[]{:S(2)}, u32[]{:S(2)}) collective-permute-start(bf16[64,2048]{1,0:T(8,128)(2,1)S(1)} %pad_maximum_fusion.6), channel_id=1, source_target_pairs={{1,4},{3,6},{4,1},{6,3},{9,12},{11,14},{12,9},{14,11},{17,20},{19,... | collective-permute-start | bytes 786440 | tf_op jit(solution)/shard_map/arr2/ppermute | solution.py:91
  73.6 15.6 %collective-permute-start.14 = (bf16[64,2048]{1,0:T(8,128)(2,1)S(1)}, bf16[64,2048]{1,0:T(8,128)(2,1)S(1)}, u32[]{:S(2)}, u32[]{:S(2)}) collective-permute-start(bf16[64,2048]{1,0:T(8,128)(2,1)S(1)} %pad_maximum_fusion.6), channel_id=1, source_target_pairs={{0,4},{1,0},{2,6},{3,2},{4,5},{5,1},{6,7},{7,3},{8,12},{9,8},{10,1... | collective-permute-start | bytes 786440 | tf_op jit(solution)/shard_map/arr2/ppermute | solution.py:91
  73.6 9.8 %collective-permute-start.16 = (bf16[1,2,256,1024]{3,2,1,0:T(8,128)(2,1)S(1)}, bf16[1,2,256,1024]{3,2,1,0:T(8,128)(2,1)S(1)}, u32[]{:S(2)}, u32[]{:S(2)}) collective-permute-start(bf16[1,2,256,1024]{3,2,1,0:T(8,128)(2,1)S(1)} %c1.1), channel_id=1, source_target_pairs={{0,1},{1,0},{2,3},{3,2},{4,5},{5,4},{6,7},{7,6},{8,9},{9,8},{10,11... | collective-permute-start | bytes 3145736 | tf_op jit(solution)/shard_map/c1/ppermute | solution.py:67
  76.1 19.0 %collective-permute-start.18 = (bf16[128,1024]{1,0:T(8,128)(2,1)S(1)}, bf16[128,1024]{1,0:T(8,128)(2,1)S(1)}, u32[]{:S(2)}, u32[]{:S(2)}) collective-permute-start(bf16[128,1024]{1,0:T(8,128)(2,1)S(1)} %fusion.7.one), channel_id=1, source_target_pairs={{0,1},{1,0},{2,3},{3,2},{4,5},{5,4},{6,7},{7,6},{8,9},{9,8},{10,11... | collective-permute-start | bytes 786440 | tf_op jit(solution)/shard_map/hide0/ppermute | solution.py:67
  76.2 29.5 %collective-permute-start.13 = (bf16[128,1024]{1,0:T(8,128)(2,1)S(1)}, bf16[128,1024]{1,0:T(8,128)(2,1)S(1)}, u32[]{:S(2)}, u32[]{:S(2)}) collective-permute-start(bf16[128,1024]{1,0:T(8,128)(2,1)S(1)} %fusion.7.one), channel_id=1, source_target_pairs={{0,2},{1,3},{2,0},{3,1},{4,6},{5,7},{6,4},{7,5},{8,10},{9,11},{10,... | collective-permute-start | bytes 786440 | tf_op jit(solution)/shard_map/hide0/ppermute | solution.py:67
  94.3 11.9 %collective-permute-start.19 = (bf16[1,2,128,1024]{3,2,1,0:T(8,128)(2,1)S(1)}, bf16[1,2,128,1024]{3,2,1,0:T(8,128)(2,1)S(1)}, u32[]{:S(2)}, u32[]{:S(2)}) collective-permute-start(bf16[1,2,128,1024]{3,2,1,0:T(8,128)(2,1)S(1)} %a2.1), channel_id=1, source_target_pairs={{0,1},{1,0},{2,3},{3,2},{4,5},{5,4},{6,7},{7,6},{8,9},{9,8},{10,11... | collective-permute-start | bytes 1572872 | tf_op jit(solution)/shard_map/a2/ppermute | solution.py:67
  105.5 15.0 %collective-permute-start.22 = (bf16[1,2,128,1024]{3,2,1,0:T(8,128)(2,1)S(1)}, bf16[1,2,128,1024]{3,2,1,0:T(8,128)(2,1)S(1)}, u32[]{:S(2)}, u32[]{:S(2)}) collective-permute-start(bf16[1,2,128,1024]{3,2,1,0:T(8,128)(2,1)S(1)} %c2.1), channel_id=1, source_target_pairs={{0,1},{1,0},{2,3},{3,2},{4,5},{5,4},{6,7},{7,6},{8,9},{9,8},{10,11... | collective-permute-start | bytes 1572872 | tf_op jit(solution)/shard_map/c2/ppermute | solution.py:67
  105.6 24.3 %collective-permute-start.25 = (bf16[1,2,256,1024]{3,2,1,0:T(8,128)(2,1)S(1)}, bf16[1,2,256,1024]{3,2,1,0:T(8,128)(2,1)S(1)}, u32[]{:S(2)}, u32[]{:S(2)}) collective-permute-start(bf16[1,2,256,1024]{3,2,1,0:T(8,128)(2,1)S(1)} %b1.1), channel_id=1, source_target_pairs={{0,2},{1,3},{2,0},{3,1},{4,6},{5,7},{6,4},{7,5},{8,10},{9,11},{10,... | collective-permute-start | bytes 3145736 | tf_op jit(solution)/shard_map/b1/ppermute | solution.py:67
  116.7 8.8 %collective-permute-start.21 = (bf16[64,2048]{1,0:T(8,128)(2,1)S(1)}, bf16[64,2048]{1,0:T(8,128)(2,1)S(1)}, u32[]{:S(2)}, u32[]{:S(2)}) collective-permute-start(bf16[64,2048]{1,0:T(8,128)(2,1)S(1)} %get-tuple-element.107), channel_id=1, source_target_pairs={{0,1},{1,5},{2,3},{3,7},{4,0},{5,4},{6,2},{7,6},{8,9},{9,13},{10,1... | collective-permute-start | bytes 786440 | tf_op jit(solution)/shard_map/out0/ppermute | solution.py:91
  116.8 8.8 %collective-permute-start.23 = (bf16[64,2048]{1,0:T(8,128)(2,1)S(1)}, bf16[64,2048]{1,0:T(8,128)(2,1)S(1)}, u32[]{:S(2)}, u32[]{:S(2)}) collective-permute-start(bf16[64,2048]{1,0:T(8,128)(2,1)S(1)} %get-tuple-element.106), channel_id=1, source_target_pairs={{1,4},{3,6},{4,1},{6,3},{9,12},{11,14},{12,9},{14,11},{17,20},{19,... | collective-permute-start | bytes 786440 | tf_op jit(solution)/shard_map/out0/ppermute | solution.py:91
  132.8 13.5 %collective-permute-start.27 = (bf16[1,2,128,1024]{3,2,1,0:T(8,128)(2,1)S(1)}, bf16[1,2,128,1024]{3,2,1,0:T(8,128)(2,1)S(1)}, u32[]{:S(2)}, u32[]{:S(2)}) collective-permute-start(bf16[1,2,128,1024]{3,2,1,0:T(8,128)(2,1)S(1)} %b2.1), channel_id=1, source_target_pairs={{0,2},{1,3},{2,0},{3,1},{4,6},{5,7},{6,4},{7,5},{8,10},{9,11},{10,... | collective-permute-start | bytes 1572872 | tf_op jit(solution)/shard_map/b2/ppermute | solution.py:67
  132.8 15.3 %collective-permute-start.26 = (bf16[32,2048]{1,0:T(8,128)(2,1)S(1)}, bf16[32,2048]{1,0:T(8,128)(2,1)S(1)}, u32[]{:S(2)}, u32[]{:S(2)}) collective-permute-start(bf16[32,2048]{1,0:T(8,128)(2,1)S(1)} %get-tuple-element.98), channel_id=1, source_target_pairs={{0,8},{4,12},{8,0},{12,4},{1,9},{5,13},{9,1},{13,5},{2,10},{6,14},... | collective-permute-start | bytes 393224 | tf_op jit(solution)/shard_map/far_out0/ppermute | solution.py:71
  134.9 22.6 %collective-permute-start.29 = (bf16[256,1024]{1,0:T(8,128)(2,1)S(1)}, bf16[256,1024]{1,0:T(8,128)(2,1)S(1)}, u32[]{:S(2)}, u32[]{:S(2)}) collective-permute-start(bf16[256,1024]{1,0:T(8,128)(2,1)S(1)} %fusion.2.one), channel_id=1, source_target_pairs={{0,2},{1,3},{2,0},{3,1},{4,6},{5,7},{6,4},{7,5},{8,10},{9,11},{10,... | collective-permute-start | bytes 1572872 | tf_op jit(solution)/shard_map/hide1/ppermute | solution.py:67
  146.6 26.0 %collective-permute-start.33 = (bf16[128,1024]{1,0:T(8,128)(2,1)S(1)}, bf16[128,1024]{1,0:T(8,128)(2,1)}, u32[]{:S(2)}, u32[]{:S(2)}) collective-permute-start(bf16[128,1024]{1,0:T(8,128)(2,1)S(1)} %fusion.5.one), channel_id=1, source_target_pairs={{0,2},{1,3},{2,0},{3,1},{4,6},{5,7},{6,4},{7,5},{8,10},{9,11},{10,... | collective-permute-start | bytes 786440 | tf_op jit(solution)/shard_map/hide2/ppermute | solution.py:67
  146.8 12.0 %collective-permute-start.30 = (bf16[128,1024]{1,0:T(8,128)(2,1)S(1)}, bf16[128,1024]{1,0:T(8,128)(2,1)S(1)}, u32[]{:S(2)}, u32[]{:S(2)}) collective-permute-start(bf16[128,1024]{1,0:T(8,128)(2,1)S(1)} %fusion.5.one), channel_id=1, source_target_pairs={{0,1},{1,0},{2,3},{3,2},{4,5},{5,4},{6,7},{7,6},{8,9},{9,8},{10,11... | collective-permute-start | bytes 786440 | tf_op jit(solution)/shard_map/hide2/ppermute | solution.py:67
  173.4 11.7 %collective-permute-start.32 = (bf16[128,2048]{1,0:T(8,128)(2,1)}, bf16[128,2048]{1,0:T(8,128)(2,1)S(1)}, u32[]{:S(2)}, u32[]{:S(2)}) collective-permute-start(bf16[128,2048]{1,0:T(8,128)(2,1)} %get-tuple-element.101), channel_id=1, source_target_pairs={{0,1},{1,5},{2,3},{3,7},{4,0},{5,4},{6,2},{7,6},{8,9},{9,13},{10,1... | collective-permute-start | bytes 1572872 | tf_op jit(solution)/shard_map/out1/ppermute | solution.py:91
  173.4 14.8 %collective-permute-start.35 = (bf16[128,2048]{1,0:T(8,128)(2,1)}, bf16[128,2048]{1,0:T(8,128)(2,1)S(1)}, u32[]{:S(2)}, u32[]{:S(2)}) collective-permute-start(bf16[128,2048]{1,0:T(8,128)(2,1)} %get-tuple-element.100), channel_id=1, source_target_pairs={{1,4},{3,6},{4,1},{6,3},{9,12},{11,14},{12,9},{14,11},{17,20},{19,... | collective-permute-start | bytes 1572872 | tf_op jit(solution)/shard_map/out1/ppermute | solution.py:91
  183.1 8.3 %collective-permute-start.38 = (bf16[64,2048]{1,0:T(8,128)(2,1)S(1)}, bf16[64,2048]{1,0:T(8,128)(2,1)S(1)}, u32[]{:S(2)}, u32[]{:S(2)}) collective-permute-start(bf16[64,2048]{1,0:T(8,128)(2,1)S(1)} %get-tuple-element.105), channel_id=1, source_target_pairs={{1,4},{3,6},{4,1},{6,3},{9,12},{11,14},{12,9},{14,11},{17,20},{19,... | collective-permute-start | bytes 786440 | tf_op jit(solution)/shard_map/out2/ppermute | solution.py:91
  194.5 16.8 %collective-permute-start.39 = (bf16[64,2048]{1,0:T(8,128)(2,1)S(1)}, bf16[64,2048]{1,0:T(8,128)(2,1)S(1)}, u32[]{:S(2)}, u32[]{:S(2)}) collective-permute-start(bf16[64,2048]{1,0:T(8,128)(2,1)S(1)} %get-tuple-element.96), channel_id=1, source_target_pairs={{0,8},{4,12},{8,0},{12,4},{1,9},{5,13},{9,1},{13,5},{2,10},{6,14},... | collective-permute-start | bytes 786440 | tf_op jit(solution)/shard_map/far_out1/ppermute | solution.py:71
  196.1 18.1 %collective-permute-start.41 = (bf16[32,2048]{1,0:T(8,128)(2,1)S(1)}, bf16[32,2048]{1,0:T(8,128)(2,1)S(1)}, u32[]{:S(2)}, u32[]{:S(2)}) collective-permute-start(bf16[32,2048]{1,0:T(8,128)(2,1)S(1)} %get-tuple-element.94), channel_id=1, source_target_pairs={{0,8},{4,12},{8,0},{12,4},{1,9},{5,13},{9,1},{13,5},{2,10},{6,14},... | collective-permute-start | bytes 393224 | tf_op jit(solution)/shard_map/far_out2/ppermute | solution.py:71
  (15 other events, 102.9 us)
